TPU v7x, 128 devices: a whole 4x4x4 slice. The times are simulated.
128 devices in a mesh: tm: 4 (over z_hi, core), rows: 4 (over y), heads: 8 (over z_lo, x).
Axes of the slice: x: 4, y: 4, z: 4 (z_hi: 2, z_lo: 2; z = z_hi * 2 + z_lo), core: 2. Of those that a mesh axis runs over, the one named last changes fastest.
Arguments:
- queries: bfloat16 [4, 4, 3, 8, 256, 128], P('tm', 'rows', None, 'heads'), parts along dimension 3, may hold values from -8 to 8
- keys: bfloat16 [4, 4, 3, 8, 256, 128], P('tm', 'rows', None, 'heads'), parts along dimension 3, may hold values from -8 to 8
- values: bfloat16 [4, 4, 3, 8, 256, 128], P('tm', 'rows', None, 'heads'), parts along dimension 3, may hold values from -6 to 6
- d_out: bfloat16 [4, 4, 3, 8, 256, 128], P('tm', 'rows', None, 'heads'), parts along dimension 3, may hold values from -6 to 6
- window_mask: int32 [4, 4, 3, 8, 27], P('tm', 'rows', None, 'heads'), parts along dimension 3, may hold values from 0 to 1, as said below
Outputs:
- attended: bfloat16 [4, 4, 3, 8, 256, 128], P('tm', 'rows', None, 'heads'), parts along dimension 3
- grad_q: bfloat16 [4, 4, 3, 8, 256, 128], P('tm', 'rows', None, 'heads'), parts along dimension 3
- grad_k: bfloat16 [4, 4, 3, 8, 256, 128], P('tm', 'rows', None, 'heads'), parts along dimension 3
- grad_v: bfloat16 [4, 4, 3, 8, 256, 128], P('tm', 'rows', None, 'heads'), parts along dimension 3
There are 8 independent parts, one for each index of `heads`. A program takes and returns all parts, laid end to end along the dimension named above; each array names one. Nothing has to cross between parts.
Inputs may be any that keep to these rules, and one draw needn't show every extreme that they name: `window_mask`: an entry is 0 wherever the offset tile lies outside the grid, the centre entry (index 13) is always 1, and the mask is symmetric: the entry of tile g at offset o equals the entry of tile g + o at offset -o.
All inputs are finite; a program needn't handle non-finite values.
Results may differ from a plain program's by a relative error of at most 0.013.
Values may be sent and summed in bfloat16 or wider, within the bound.
No kernel may reach another device: no remote copies, remote signals or barrier semaphores. Data moves between devices by JAX's collectives and lax.ppermute only.
A program may use at most 64 MiB of HBM per device.

v0:
```python
import math

import jax
import jax.numpy as jnp
from jax import lax
from jax.experimental import pallas as pl
from jax.experimental.pallas import tpu as pltpu
from jax.sharding import PartitionSpec as P

TM, ROWS = "tm", "rows"
F32, BF16 = jnp.float32, jnp.bfloat16
SLOTS = 9
ROOM = 32
GROUP = 12
LIST = 28
BIG = 6
ROW_STEPS = (0, -1, 1)
NT = (((1,), (1,)), ((), ()))
NN = (((1,), (0,)), ((), ()))


def dot(left, right, dims):
    return lax.dot_general(left, right, dims, preferred_element_type=F32)


def find_pairs(mask, lists, columns):
    near = 1 - 2 * lax.rem(lax.axis_index(TM), 2)
    frame_steps = (0, near, -near)
    n = jnp.int32(0)
    for slot in range(SLOTS):
        dt, dr = frame_steps[slot // 3], ROW_STEPS[slot % 3]
        for c in range(columns):
            for other in range(max(c - 1, 0), min(c + 2, columns)):
                lists[n] = ROOM * c + slot * columns + other
                n = n + mask[0, 0, c, 0, 9 * (dt + 1) + 3 * (dr + 1) + other - c + 1]
    for extra in range(GROUP - 1):
        lists[n + extra] = ROOM * columns
    lists[list_size(columns) - 1] = (n + GROUP - 1) // GROUP


def find_column_pairs(mask, lists, columns):
    near = 1 - 2 * lax.rem(lax.axis_index(TM), 2)
    frame_steps = (0, near, -near)
    for c in range(columns):
        n = jnp.int32(0)
        for slot in range(SLOTS):
            dt, dr = frame_steps[slot // 3], ROW_STEPS[slot % 3]
            for other in range(max(c - 1, 0), min(c + 2, columns)):
                lists[c * LIST + n] = slot * columns + other
                n = n + mask[0, 0, c, 0, 9 * (dt + 1) + 3 * (dr + 1) + other - c + 1]
        lists[c * LIST + n] = c
        lists[columns * LIST + c] = n


def list_size(columns):
    return 27 * columns + GROUP


def pack_kernel(columns, mask, q, k, v, g, kv, qg, pairs, column_pairs):
    kv[0], kv[1], qg[0], qg[1] = k[...], v[...], q[...], g[...]
    find_pairs(mask, pairs, columns)
    find_column_pairs(mask, column_pairs, columns)


def fetch(own, slots, near, mine, sems):
    tokens = own[0].shape[0]
    copies = []
    for i in range(4):
        to = near if i < 2 else mine
        copies.append(pltpu.make_async_copy(own[i], to.at[i % 2, pl.ds(0, tokens)], sems.at[i]))
    for s in range(1, SLOTS):
        at = pl.ds(s * tokens, tokens)
        halves = len(slots) - SLOTS + 1
        if s <= len(slots) - 2 * halves:
            copies.append(pltpu.make_async_copy(slots[s - 1], near.at[:, at], sems.at[s + 3]))
        else:
            for i in range(2):
                n = 2 * s + i - SLOTS + halves - 1
                copies.append(pltpu.make_async_copy(slots[n], near.at[i, at], sems.at[n + 4]))
    for copy in copies:
        copy.start()
    return copies


def for_groups(columns, lists, run):
    def step(i, carry):
        at = [GROUP * i + j for j in range(GROUP)]
        entries = [lists[place] for place in at]
        run(at, [entry // ROOM for entry in entries], [lax.rem(entry, ROOM) for entry in entries])
        return carry

    lax.fori_loop(0, lists[list_size(columns) - 1], step, 0)


def query_kernel(columns, tile, scale, lists, *refs):
    own, slots = refs[:4], refs[4:SLOTS + 6]
    out, grad_q, stats = refs[SLOTS + 6:SLOTS + 9]
    near, mine, s_all, w_all, top, low, acc, sems = refs[SLOTS + 9:]
    copies = fetch(own, slots, near, mine, sems)
    unit = scale * math.log2(math.e)
    top[...] = jnp.full(top.shape, -jnp.inf, F32)
    low[...] = jnp.zeros(low.shape, F32)
    acc[...] = jnp.zeros(acc.shape, F32)
    for copy in copies:
        copy.wait()

    def rows(index):
        return pl.ds(pl.multiple_of(index * tile, tile), tile)

    def wide(x):
        return jnp.concatenate([x, x], 1)

    def score_step(at, ours, tiles):
        for place, c, t in zip(at, ours, tiles):
            s = dot(mine[0, rows(c), :], near[0, rows(t), :], NT) * unit
            s_all[place] = s
            top[rows(c), :] = jnp.maximum(top[rows(c), :], jnp.maximum(s[:, :128], s[:, 128:]))

    for_groups(columns, lists, score_step)
    for c in range(columns):
        own_rows = slice(c * tile, (c + 1) * tile)
        peak = jnp.max(top[own_rows, :], axis=1, keepdims=True)
        top[own_rows, :] = jnp.broadcast_to(peak, (tile, 128))

    def value_step(at, ours, tiles):
        for place, c, t in zip(at, ours, tiles):
            v = near[1, rows(t), :]
            e = jnp.exp2(s_all[place] - wide(top[rows(c), :]))
            s_all[place] = e
            w_all[place] = dot(mine[1, rows(c), :], v, NT)
            low[rows(c), :] += e[:, :128] + e[:, 128:]
            acc[rows(c), :] += dot(e.astype(BF16), v, NN)

    for_groups(columns, lists, value_step)
    lane = lax.broadcasted_iota(jnp.int32, (tile, 128), 1)
    for c in range(columns):
        own_rows = slice(c * tile, (c + 1) * tile)
        total = jnp.sum(low[own_rows, :], axis=1, keepdims=True)
        inverse = 1.0 / total
        attended = (acc[own_rows, :] * inverse).astype(BF16)
        out[own_rows, :] = attended
        delta = jnp.sum(mine[1, own_rows, :].astype(F32) * attended.astype(F32), axis=1, keepdims=True)
        both = jnp.where(lane == 0, top[own_rows, :] + jnp.log2(total), delta).T
        stats[c:c + 1, :] = both[0:1]
        stats[4 + c:5 + c, :] = both[1:2]
        top[own_rows, :] = jnp.broadcast_to(delta, (tile, 128))
        low[own_rows, :] = jnp.broadcast_to(inverse * scale, (tile, 128))
        acc[own_rows, :] = jnp.zeros((tile, 128), F32)

    def query_step(at, ours, tiles):
        for place, c, t in zip(at, ours, tiles):
            ds = s_all[place] * (w_all[place] - wide(top[rows(c), :]))
            acc[rows(c), :] += dot(ds.astype(BF16), near[0, rows(t), :], NN)

    for_groups(columns, lists, query_step)
    grad_q[...] = (acc[:columns * tile, :] * low[:columns * tile, :]).astype(BF16)


def grouped(n, run):
    many = n // BIG

    def big(i, carry):
        run(BIG * i, BIG)
        return carry

    def small(i, carry):
        run(BIG * many + 2 * i, 2)
        return carry

    lax.fori_loop(0, many, big, 0)
    lax.fori_loop(0, (n - BIG * many + 1) // 2, small, 0)


def key_kernel(columns, tile, scale, lists, *refs):
    own, slots, sets = refs[:4], refs[4:SLOTS + 6], refs[SLOTS + 6:SLOTS + 9]
    grad_k, grad_v, near, mine, logs, deltas, k_acc, v_acc, sems = refs[SLOTS + 9:]
    copies = fetch(own, slots, near, mine, sems)
    for slot in range(SLOTS):
        first = 8 * (slot // 3)
        logs[slot * columns:(slot + 1) * columns, :] = sets[slot % 3][first:first + columns, :]
        deltas[slot * columns:(slot + 1) * columns, :] = sets[slot % 3][first + 4:first + 4 + columns, :]
    logs[SLOTS * columns:, :] = jnp.full((5, tile), 1e30, F32)
    for copy in copies:
        copy.wait()
    unit = scale * math.log2(math.e)

    def one_column(c, carry):
        rows = pl.ds(pl.multiple_of(c * tile, tile), tile)
        n = lists[columns * LIST + c]
        k_acc[...] = jnp.zeros(k_acc.shape, F32)
        v_acc[...] = jnp.zeros(v_acc.shape, F32)

        def step(first, size):
            k = mine[0, rows, :]
            v = mine[1, rows, :]
            sum_v = v_acc[...]
            sum_k = k_acc[...]
            for j in range(size):
                t = lists[c * LIST + first + j]
                at = pl.ds(pl.multiple_of(t * tile, tile), tile)
                q, g = near[0, at, :], near[1, at, :]
                held = jnp.where(first + j < n, t, SLOTS * columns) if size == 2 and j == 1 else t
                log_total = logs[pl.ds(held, 1), :]
                delta = deltas[pl.ds(t, 1), :]
                p = jnp.exp2(dot(k, q, NT) * unit - log_total)
                sum_v = sum_v + dot(p.astype(BF16), g, NN)
                ds = p * (dot(v, g, NT) - delta)
                sum_k = sum_k + dot(ds.astype(BF16), q, NN)
            v_acc[...] = sum_v
            k_acc[...] = sum_k

        grouped(n, step)
        grad_k[rows, :] = (k_acc[...] * scale).astype(BF16)
        grad_v[rows, :] = v_acc[...].astype(BF16)
        return carry

    lax.fori_loop(0, columns, one_column, 0)


def ring(axis, step):
    count = lax.axis_size(axis)
    return [(i, (i + step) % count) for i in range(count)]


def pair_up(axis, first):
    count = lax.axis_size(axis)
    to = list(range(count))
    for i in range(first, count - 1, 2):
        to[i], to[i + 1] = i + 1, i
    return list(enumerate(to))


def moves():
    return ring(ROWS, 1), ring(ROWS, -1), pair_up(TM, 0), pair_up(TM, 1)


def spread_small(x):
    before, after, near, far = moves()
    frames = jnp.concatenate([x, lax.ppermute(x, TM, near), lax.ppermute(x, TM, far)], 0)
    return [frames, lax.ppermute(frames, ROWS, before), lax.ppermute(frames, ROWS, after)]


def then(first, *values):
    return lax.optimization_barrier((first, *values))


ANY = pl.BlockSpec(memory_space=pl.ANY)
VMEM = pl.BlockSpec(memory_space=pltpu.VMEM)
HBM = pl.BlockSpec(memory_space=pltpu.HBM)
SMEM = pl.BlockSpec(memory_space=pltpu.SMEM)
PARAMS = pltpu.CompilerParams(vmem_limit_bytes=52 * 2**20)


def query_call(columns, lists, q, k, v, g, near_kv, scale):
    tokens, width = q.shape
    tile = tokens // columns
    field = jax.ShapeDtypeStruct((tokens, width), BF16)
    total = pltpu.VMEM(((columns + 1) * tile, width), F32)
    squares = pltpu.VMEM((list_size(columns) - 18, tile, tile), F32)
    return pl.pallas_call(
        lambda *refs: query_kernel(columns, tile, scale, *refs),
        out_shape=(field, field, jax.ShapeDtypeStruct((8, tile), F32)),
        in_specs=[SMEM] + [HBM] * 4 + [ANY] * (SLOTS + 2),
        out_specs=(VMEM, VMEM, VMEM),
        scratch_shapes=[
            pltpu.VMEM((2, SLOTS * tokens, width), BF16),
            pltpu.VMEM((2, tokens + tile, width), BF16),
            squares, squares,
            total, total, total,
            pltpu.SemaphoreType.DMA((SLOTS + 6,)),
        ],
        compiler_params=PARAMS,
        cost_estimate=pl.CostEstimate(
            flops=32 * 5 * 2 * tile * tile * width, bytes_accessed=8 * tokens * width, transcendentals=32 * tile * tile
        ),
        name="query_side",
    )(lists, k, v, q, g, *near_kv)


def key_call(columns, lists, q, k, v, g, near_qg, near_stats, scale):
    tokens, width = q.shape
    tile = tokens // columns
    field = jax.ShapeDtypeStruct((tokens, width), BF16)
    total = pltpu.VMEM((tile, width), F32)
    return pl.pallas_call(
        lambda *refs: key_kernel(columns, tile, scale, *refs),
        out_shape=(field, field),
        in_specs=[SMEM] + [HBM] * 4 + [ANY] * (SLOTS + 2) + [VMEM] * 3,
        out_specs=(VMEM, VMEM),
        scratch_shapes=[
            pltpu.VMEM((2, SLOTS * tokens, width), BF16),
            pltpu.VMEM((2, tokens + tile, width), BF16),
            *[pltpu.VMEM((SLOTS * columns + 5, tile), F32)] * 2,
            total, total,
            pltpu.SemaphoreType.DMA((SLOTS + 6,)),
        ],
        compiler_params=PARAMS,
        cost_estimate=pl.CostEstimate(
            flops=32 * 4 * 2 * tile * tile * width, bytes_accessed=8 * tokens * width, transcendentals=32 * tile * tile
        ),
        name="key_side",
    )(lists, q, g, k, v, *near_qg, *near_stats)


def body(queries, keys, values, d_out, window_mask):
    columns, tile, width = queries.shape[2], queries.shape[4], queries.shape[5]
    tokens = columns * tile
    scale = width ** -0.5
    flat = lambda x: x.reshape(tokens, width)
    pair = jax.ShapeDtypeStruct((2, tokens, width), BF16)
    own = [flat(x) for x in (queries, keys, values, d_out)]
    kv, qg, pairs, column_pairs = pl.pallas_call(
        lambda *refs: pack_kernel(columns, *refs),
        out_shape=(
            pair, pair,
            jax.ShapeDtypeStruct((list_size(columns),), jnp.int32),
            jax.ShapeDtypeStruct((columns * (LIST + 1),), jnp.int32),
        ),
        in_specs=[SMEM] + [VMEM] * 4,
        out_specs=(VMEM, VMEM, SMEM, SMEM),
        name="pack",
    )(window_mask, *own)
    before, after, near, far = moves()
    send = lax.ppermute
    kv_o = send(kv, TM, near)
    kv_up, kv_down = send(kv, ROWS, before), send(kv, ROWS, after)
    frame = lax.axis_index(TM)
    inner = (frame > 0) & (frame < lax.axis_size(TM) - 1)
    half = send(jnp.where(inner, kv[0], kv_o[1]), TM, ring(TM, 2))
    qg_o = send(qg, TM, near)
    qg_half = send(jnp.where(inner, qg[0], qg_o[1]), TM, ring(TM, 2))
    half, qg_next = then(half, qg)
    half_up, half_down = send(half, ROWS, before), send(half, ROWS, after)
    rest = send(half, TM, near)
    kv_ou, kv_od = send(kv_up, TM, near), send(kv_down, TM, near)
    qg_up, qg_down = send(qg_next, ROWS, before), send(qg_next, ROWS, after)
    qg_half, half_up, half_down = then(qg_half, half_up, half_down)
    rest_up, rest_down = send(half_up, TM, near), send(half_down, TM, near)
    qg_half_up, qg_half_down = send(qg_half, ROWS, before), send(qg_half, ROWS, after)
    near_kv = [kv_up, kv_down, kv_o, kv_ou, kv_od, rest, half, rest_up, half_up, rest_down, half_down]
    attended, grad_q, stats = query_call(columns, pairs, *own, near_kv, scale)
    stats, qg_half, qg_up, qg_down, qg_half_up, qg_half_down = then(
        stats, qg_half, qg_up, qg_down, qg_half_up, qg_half_down
    )
    near_stats = spread_small(stats)
    qg_ou, qg_od = send(qg_up, TM, near), send(qg_down, TM, near)
    qg_rest, qg_rest_up, qg_rest_down = [send(x, TM, near) for x in (qg_half, qg_half_up, qg_half_down)]
    near_qg = [
        qg_up, qg_down, qg_o, qg_ou, qg_od, qg_rest, qg_half, qg_rest_up, qg_half_up, qg_rest_down, qg_half_down
    ]
    grad_k, grad_v = key_call(columns, column_pairs, *own, near_qg, near_stats, scale)
    return tuple(x.reshape(queries.shape) for x in (attended, grad_q, grad_k, grad_v))


def solution(mesh):
    field = P(TM, ROWS, None, "heads", None, None)
    return jax.shard_map(
        body,
        mesh=mesh,
        in_specs=(field, field, field, field, P(TM, ROWS, None, "heads", None)),
        out_specs=(field, field, field, field),
        check_vma=False,
    )
```

profile of v0, /device:TPU:112, one launch (start us, length us, event | category | flops | bytes accessed | tf_op | source)
XLA Modules:
  0.0 71.4 jit_solution(2128913270380796399)
XLA Ops:
  0.6 2.2 %pack.1 = (bf16[2,768,128]{2,1,0:T(8,128)(2,1)}, bf16[2,768,128]{2,1,0:T(8,128)(2,1)}, s32[93]{0:T(128)}, s32[87]{0:T(128)}) custom-call(s32[1,1,3,1,27]{4,3,2,1,0:T(1,128)} %refs_0_.1, bf16[768,128]{1,0:T(8,128)(2,1)} %bitcast.20, bf16[768,128]{1,0:T(8,128)(2,1)} %bitcast.23, bf16[768,128]{1,0:T(8,128)(2,1)} %bitcast.26, bf16[768,128]{1,0:T(8,128)(2,1)} %bitcast.29), custom_call_target="tpu_custom_call" | custom-call | tf_op jit(solution)/shard_map/pack/pallas_call | solution.py:312
  2.9 0.5 collective-permute-start.7
  3.4 1.3 %collective-permute-start = (bf16[2,768,128]{2,1,0:T(8,128)(2,1)}, bf16[2,768,128]{2,1,0:T(8,128)(2,1)S(1)}, u32[]{:S(2)}, u32[]{:S(2)}) collective-permute-start(bf16[2,768,128]{2,1,0:T(8,128)(2,1)} %get-tuple-element.25), channel_id=1, source_target_pairs={{0,8},{8,16},{16,24},{24,0},{1,9},{9,17},{17,25},{25,1},{2,10},{10... | collective-permute-start | bytes 1179656 | tf_op jit(solution)/shard_map/ppermute | solution.py:326
  4.7 0.7 %collective-permute-start.1 = (bf16[2,768,128]{2,1,0:T(8,128)(2,1)}, bf16[2,768,128]{2,1,0:T(8,128)(2,1)S(1)}, u32[]{:S(2)}, u32[]{:S(2)}) collective-permute-start(bf16[2,768,128]{2,1,0:T(8,128)(2,1)} %get-tuple-element.25), channel_id=1, source_target_pairs={{0,24},{8,0},{16,8},{24,16},{1,25},{9,1},{17,9},{25,17},{2,26},{10... | collective-permute-start | bytes 1179656 | tf_op jit(solution)/shard_map/ppermute | solution.py:326
  5.4 1.1 %fusion.1 = bf16[768,128]{1,0:T(8,128)(2,1)S(1)} fusion(bf16[2,768,128]{2,1,0:T(8,128)(2,1)S(1)} %collective-permute-done.2.refs_7_, bf16[2,768,128]{2,1,0:T(8,128)(2,1)} %get-tuple-element.25, pred[]{:T(512)S(6)} %and.4), kind=kLoop, calls=%fused_computation.3 | loop fusion | flops 98304 | bytes 589825 | tf_op jit(solution)/shard_map/jit(_where)/select_n | solution.py:329
  6.6 0.6 collective-permute-start.5
  7.3 3.1 %collective-permute-start.8 = (bf16[768,128]{1,0:T(8,128)(2,1)S(1)}, bf16[768,128]{1,0:T(8,128)(2,1)S(1)}, u32[]{:S(2)}, u32[]{:S(2)}) collective-permute-start(bf16[768,128]{1,0:T(8,128)(2,1)S(1)} %fusion), channel_id=1, source_target_pairs={{0,64},{32,96},{64,0},{96,32},{1,65},{33,97},{65,1},{97,33},{2,66}... | collective-permute-start | bytes 589832 | tf_op jit(solution)/shard_map/ppermute | solution.py:331
  10.3 4.4 %collective-permute-done.refs_5_ = bf16[2,768,128]{2,1,0:T(8,128)(2,1)S(1)} collective-permute-done((bf16[2,768,128]{2,1,0:T(8,128)(2,1)}, bf16[2,768,128]{2,1,0:T(8,128)(2,1)S(1)}, u32[]{:S(2)}, u32[]{:S(2)}) %collective-permute-start) | collective-permute-done | bytes 393248 | tf_op jit(solution)/shard_map/ppermute | solution.py:326
  14.7 1.3 %collective-permute-done.5.refs_11_ = bf16[768,128]{1,0:T(8,128)(2,1)S(1)} collective-permute-done((bf16[768,128]{1,0:T(8,128)(2,1)S(1)}, bf16[768,128]{1,0:T(8,128)(2,1)S(1)}, u32[]{:S(2)}, u32[]{:S(2)}) %collective-permute-start.5) | collective-permute-done | bytes 196640 | tf_op jit(solution)/shard_map/ppermute | solution.py:329
  16.4 1.6 %collective-permute-start.9 = (bf16[768,128]{1,0:T(8,128)(2,1)S(1)}, bf16[768,128]{1,0:T(8,128)(2,1)S(1)}, u32[]{:S(2)}, u32[]{:S(2)}) collective-permute-start(bf16[768,128]{1,0:T(8,128)(2,1)S(1)} %collective-permute-done.5.refs_11_), channel_id=1, source_target_pairs={{0,8},{8,16},{16,24},{24,0},{1,9},{9,17},{17,25},{25,1},{2,10},{10... | collective-permute-start | bytes 589832 | tf_op jit(solution)/shard_map/ppermute | solution.py:333
  18.0 0.7 collective-permute-done.8.refs_11_
  18.7 3.3 %collective-permute-done.10.refs_15_ = bf16[768,128]{1,0:T(8,128)(2,1)S(1)} collective-permute-done((bf16[768,128]{1,0:T(8,128)(2,1)S(1)}, bf16[768,128]{1,0:T(8,128)(2,1)S(1)}, u32[]{:S(2)}, u32[]{:S(2)}) %collective-permute-start.10) | collective-permute-done | bytes 196640 | tf_op jit(solution)/shard_map/ppermute | solution.py:333
  22.2 0.5 collective-permute-start.12
  22.7 2.3 %collective-permute-start.13 = (bf16[2,768,128]{2,1,0:T(8,128)(2,1)S(1)}, bf16[2,768,128]{2,1,0:T(8,128)(2,1)S(1)}, u32[]{:S(2)}, u32[]{:S(2)}) collective-permute-start(bf16[2,768,128]{2,1,0:T(8,128)(2,1)S(1)} %copy-done.7), channel_id=1, source_target_pairs={{0,8},{8,16},{16,24},{24,0},{1,9},{9,17},{17,25},{25,1},{2,10},{10... | collective-permute-start | bytes 1179656 | tf_op jit(solution)/shard_map/ppermute | solution.py:336
  25.1 3.0 %collective-permute-start.15 = (bf16[768,128]{1,0:T(8,128)(2,1)S(1)}, bf16[768,128]{1,0:T(8,128)(2,1)S(1)}, u32[]{:S(2)}, u32[]{:S(2)}) collective-permute-start(bf16[768,128]{1,0:T(8,128)(2,1)S(1)} %collective-permute-done.8.refs_11_), channel_id=1, source_target_pairs={{0,8},{8,16},{16,24},{24,0},{1,9},{9,17},{17,25},{25,1},{2,10},{10... | collective-permute-start | bytes 589832 | tf_op jit(solution)/shard_map/ppermute | solution.py:339
  28.2 14.0 %query_side.1 = (bf16[768,128]{1,0:T(8,128)(2,1)}, bf16[768,128]{1,0:T(8,128)(2,1)}, f32[8,256]{1,0:T(8,128)S(1)}) custom-call(s32[93]{0:T(128)S(1)} %copy-done.5, bf16[768,128]{1,0:T(8,128)(2,1)S(1)} %bitcast.24, bf16[768,128]{1,0:T(8,128)(2,1)S(1)} %bitcast.27, bf16[768,128]{1,0:T(8,128)(2,1)S(1)} %bitcast.21, bf16[768,128]{1,0:T(8,128)(2,1)S(1)} %bitcast.30, ...), custom_call_target="tpu_custom_call" | custom-call | flops 2684354560 | bytes 786432 | tf_op jit(solution)/shard_map/query_side/pallas_call | solution.py:260
  42.4 1.9 %collective-permute-start.23 = (f32[8,256]{1,0:T(8,128)S(1)}, f32[8,256]{1,0:T(8,128)S(1)}, u32[]{:S(2)}, u32[]{:S(2)}) collective-permute-start(f32[8,256]{1,0:T(8,128)S(1)} %get-tuple-element.41), channel_id=1, source_target_pairs={{0,0},{32,64},{64,32},{96,96},{1,1},{33,65},{65,33},{97,97},{2,2},... | collective-permute-start | bytes 24584 | tf_op jit(solution)/shard_map/ppermute | solution.py:239
  44.9 4.0 %collective-permute-done.23 = f32[8,256]{1,0:T(8,128)S(1)} collective-permute-done((f32[8,256]{1,0:T(8,128)S(1)}, f32[8,256]{1,0:T(8,128)S(1)}, u32[]{:S(2)}, u32[]{:S(2)}) %collective-permute-start.23) | collective-permute-done | bytes 8224 | tf_op jit(solution)/shard_map/ppermute | solution.py:239
  48.9 1.9 %collective-permute-start.24 = (f32[24,256]{1,0:T(8,128)S(1)}, f32[24,256]{1,0:T(8,128)S(1)}, u32[]{:S(2)}, u32[]{:S(2)}) collective-permute-start(f32[24,256]{1,0:T(8,128)S(1)} %constant_dynamic-update-slice_fusion.refs_16_), channel_id=1, source_target_pairs={{0,8},{8,16},{16,24},{24,0},{1,9},{9,17},{17,25},{25,1},{2,10},{10... | collective-permute-start | bytes 73736 | tf_op jit(solution)/shard_map/ppermute | solution.py:240
  50.9 1.8 %collective-permute-done.24.refs_17_ = f32[24,256]{1,0:T(8,128)S(1)} collective-permute-done((f32[24,256]{1,0:T(8,128)S(1)}, f32[24,256]{1,0:T(8,128)S(1)}, u32[]{:S(2)}, u32[]{:S(2)}) %collective-permute-start.24) | collective-permute-done | bytes 24608 | tf_op jit(solution)/shard_map/ppermute | solution.py:240
  52.7 1.9 %collective-permute-done.25.refs_18_ = f32[24,256]{1,0:T(8,128)S(1)} collective-permute-done((f32[24,256]{1,0:T(8,128)S(1)}, f32[24,256]{1,0:T(8,128)S(1)}, u32[]{:S(2)}, u32[]{:S(2)}) %collective-permute-start.25) | collective-permute-done | bytes 24608 | tf_op jit(solution)/shard_map/ppermute | solution.py:240
  54.6 1.4 %collective-permute-done.21.refs_14_ = bf16[768,128]{1,0:T(8,128)(2,1)S(1)} collective-permute-done((bf16[768,128]{1,0:T(8,128)(2,1)S(1)}, bf16[768,128]{1,0:T(8,128)(2,1)S(1)}, u32[]{:S(2)}, u32[]{:S(2)}) %collective-permute-start.21) | collective-permute-done | bytes 196640 | tf_op jit(solution)/shard_map/ppermute | solution.py:347
  56.1 0.7 copy-done.14
  57.0 14.5 %key_side.1 = (bf16[768,128]{1,0:T(8,128)(2,1)}, bf16[768,128]{1,0:T(8,128)(2,1)}) custom-call(s32[87]{0:T(128)S(1)} %copy-done.4, bf16[768,128]{1,0:T(8,128)(2,1)S(1)} %bitcast.22, bf16[768,128]{1,0:T(8,128)(2,1)S(1)} %bitcast.31, bf16[768,128]{1,0:T(8,128)(2,1)S(1)} %bitcast.25, bf16[768,128]{1,0:T(8,128)(2,1)S(1)} %bitcast.28, ...), custom_call_target="tpu_custom_call" | custom-call | flops 2147483648 | bytes 786432 | tf_op jit(solution)/shard_map/key_side/pallas_call | solution.py:285
  (72 shorter events, 1.8 us)
Async XLA Ops:
  2.8 2.6 %collective-permute-start.2 = (bf16[2,768,128]{2,1,0:T(8,128)(2,1)}, bf16[2,768,128]{2,1,0:T(8,128)(2,1)S(1)}, u32[]{:S(2)}, u32[]{:S(2)}) collective-permute-start(bf16[2,768,128]{2,1,0:T(8,128)(2,1)} %get-tuple-element.25), channel_id=1, source_target_pairs={{0,32},{32,0},{64,96},{96,64},{1,33},{33,1},{65,97},{97,65},{2,34}... | collective-permute-start | bytes 1179656 | tf_op jit(solution)/shard_map/ppermute | solution.py:325
  2.9 4.3 %collective-permute-start.7 = (bf16[2,768,128]{2,1,0:T(8,128)(2,1)}, bf16[2,768,128]{2,1,0:T(8,128)(2,1)S(1)}, u32[]{:S(2)}, u32[]{:S(2)}) collective-permute-start(bf16[2,768,128]{2,1,0:T(8,128)(2,1)} %get-tuple-element.35), channel_id=1, source_target_pairs={{0,32},{32,0},{64,96},{96,64},{1,33},{33,1},{65,97},{97,65},{2,34}... | collective-permute-start | bytes 1179656 | tf_op jit(solution)/shard_map/ppermute | solution.py:330
  3.4 11.3 %collective-permute-start = (bf16[2,768,128]{2,1,0:T(8,128)(2,1)}, bf16[2,768,128]{2,1,0:T(8,128)(2,1)S(1)}, u32[]{:S(2)}, u32[]{:S(2)}) collective-permute-start(bf16[2,768,128]{2,1,0:T(8,128)(2,1)} %get-tuple-element.25), channel_id=1, source_target_pairs={{0,8},{8,16},{16,24},{24,0},{1,9},{9,17},{17,25},{25,1},{2,10},{10... | collective-permute-start | bytes 1179656 | tf_op jit(solution)/shard_map/ppermute | solution.py:326
  4.7 13.3 %collective-permute-start.1 = (bf16[2,768,128]{2,1,0:T(8,128)(2,1)}, bf16[2,768,128]{2,1,0:T(8,128)(2,1)S(1)}, u32[]{:S(2)}, u32[]{:S(2)}) collective-permute-start(bf16[2,768,128]{2,1,0:T(8,128)(2,1)} %get-tuple-element.25), channel_id=1, source_target_pairs={{0,24},{8,0},{16,8},{24,16},{1,25},{9,1},{17,9},{25,17},{2,26},{10... | collective-permute-start | bytes 1179656 | tf_op jit(solution)/shard_map/ppermute | solution.py:326
  6.6 9.4 %collective-permute-start.5 = (bf16[768,128]{1,0:T(8,128)(2,1)S(1)}, bf16[768,128]{1,0:T(8,128)(2,1)S(1)}, u32[]{:S(2)}, u32[]{:S(2)}) collective-permute-start(bf16[768,128]{1,0:T(8,128)(2,1)S(1)} %fusion.1), channel_id=1, source_target_pairs={{0,64},{32,96},{64,0},{96,32},{1,65},{33,97},{65,1},{97,33},{2,66}... | collective-permute-start | bytes 589832 | tf_op jit(solution)/shard_map/ppermute | solution.py:329
  7.3 11.4 %collective-permute-start.8 = (bf16[768,128]{1,0:T(8,128)(2,1)S(1)}, bf16[768,128]{1,0:T(8,128)(2,1)S(1)}, u32[]{:S(2)}, u32[]{:S(2)}) collective-permute-start(bf16[768,128]{1,0:T(8,128)(2,1)S(1)} %fusion), channel_id=1, source_target_pairs={{0,64},{32,96},{64,0},{96,32},{1,65},{33,97},{65,1},{97,33},{2,66}... | collective-permute-start | bytes 589832 | tf_op jit(solution)/shard_map/ppermute | solution.py:331
  14.7 10.3 %collective-permute-start.3 = (bf16[2,768,128]{2,1,0:T(8,128)(2,1)S(1)}, bf16[2,768,128]{2,1,0:T(8,128)(2,1)S(1)}, u32[]{:S(2)}, u32[]{:S(2)}) collective-permute-start(bf16[2,768,128]{2,1,0:T(8,128)(2,1)S(1)} %collective-permute-done.refs_5_), channel_id=1, source_target_pairs={{0,32},{32,0},{64,96},{96,64},{1,33},{33,1},{65,97},{97,65},{2,34}... | collective-permute-start | bytes 1179656 | tf_op jit(solution)/shard_map/ppermute | solution.py:335
  16.0 6.0 %collective-permute-start.10 = (bf16[768,128]{1,0:T(8,128)(2,1)S(1)}, bf16[768,128]{1,0:T(8,128)(2,1)S(1)}, u32[]{:S(2)}, u32[]{:S(2)}) collective-permute-start(bf16[768,128]{1,0:T(8,128)(2,1)S(1)} %collective-permute-done.5.refs_11_), channel_id=1, source_target_pairs={{0,24},{8,0},{16,8},{24,16},{1,25},{9,1},{17,9},{25,17},{2,26},{10... | collective-permute-start | bytes 589832 | tf_op jit(solution)/shard_map/ppermute | solution.py:333
  16.4 5.8 %collective-permute-start.9 = (bf16[768,128]{1,0:T(8,128)(2,1)S(1)}, bf16[768,128]{1,0:T(8,128)(2,1)S(1)}, u32[]{:S(2)}, u32[]{:S(2)}) collective-permute-start(bf16[768,128]{1,0:T(8,128)(2,1)S(1)} %collective-permute-done.5.refs_11_), channel_id=1, source_target_pairs={{0,8},{8,16},{16,24},{24,0},{1,9},{9,17},{17,25},{25,1},{2,10},{10... | collective-permute-start | bytes 589832 | tf_op jit(solution)/shard_map/ppermute | solution.py:333
  18.0 7.0 %collective-permute-start.4 = (bf16[2,768,128]{2,1,0:T(8,128)(2,1)S(1)}, bf16[2,768,128]{2,1,0:T(8,128)(2,1)S(1)}, u32[]{:S(2)}, u32[]{:S(2)}) collective-permute-start(bf16[2,768,128]{2,1,0:T(8,128)(2,1)S(1)} %collective-permute-done.1.refs_6_), channel_id=1, source_target_pairs={{0,32},{32,0},{64,96},{96,64},{1,33},{33,1},{65,97},{97,65},{2,34}... | collective-permute-start | bytes 1179656 | tf_op jit(solution)/shard_map/ppermute | solution.py:335
  18.7 4.0 %collective-permute-start.6 = (bf16[768,128]{1,0:T(8,128)(2,1)S(1)}, bf16[768,128]{1,0:T(8,128)(2,1)S(1)}, u32[]{:S(2)}, u32[]{:S(2)}) collective-permute-start(bf16[768,128]{1,0:T(8,128)(2,1)S(1)} %collective-permute-done.5.refs_11_), channel_id=1, source_target_pairs={{0,32},{32,0},{64,96},{96,64},{1,33},{33,1},{65,97},{97,65},{2,34}... | collective-permute-start | bytes 589832 | tf_op jit(solution)/shard_map/ppermute | solution.py:334
  22.2 5.9 %collective-permute-start.11 = (bf16[768,128]{1,0:T(8,128)(2,1)S(1)}, bf16[768,128]{1,0:T(8,128)(2,1)S(1)}, u32[]{:S(2)}, u32[]{:S(2)}) collective-permute-start(bf16[768,128]{1,0:T(8,128)(2,1)S(1)} %collective-permute-done.9.refs_13_), channel_id=1, source_target_pairs={{0,32},{32,0},{64,96},{96,64},{1,33},{33,1},{65,97},{97,65},{2,34}... | collective-permute-start | bytes 589832 | tf_op jit(solution)/shard_map/ppermute | solution.py:338
  22.2 5.9 %collective-permute-start.12 = (bf16[768,128]{1,0:T(8,128)(2,1)S(1)}, bf16[768,128]{1,0:T(8,128)(2,1)S(1)}, u32[]{:S(2)}, u32[]{:S(2)}) collective-permute-start(bf16[768,128]{1,0:T(8,128)(2,1)S(1)} %collective-permute-done.10.refs_15_), channel_id=1, source_target_pairs={{0,32},{32,0},{64,96},{96,64},{1,33},{33,1},{65,97},{97,65},{2,34}... | collective-permute-start | bytes 589832 | tf_op jit(solution)/shard_map/ppermute | solution.py:338
  22.7 19.5 %collective-permute-start.13 = (bf16[2,768,128]{2,1,0:T(8,128)(2,1)S(1)}, bf16[2,768,128]{2,1,0:T(8,128)(2,1)S(1)}, u32[]{:S(2)}, u32[]{:S(2)}) collective-permute-start(bf16[2,768,128]{2,1,0:T(8,128)(2,1)S(1)} %copy-done.7), channel_id=1, source_target_pairs={{0,8},{8,16},{16,24},{24,0},{1,9},{9,17},{17,25},{25,1},{2,10},{10... | collective-permute-start | bytes 1179656 | tf_op jit(solution)/shard_map/ppermute | solution.py:336
  25.1 17.2 %collective-permute-start.14 = (bf16[2,768,128]{2,1,0:T(8,128)(2,1)S(1)}, bf16[2,768,128]{2,1,0:T(8,128)(2,1)S(1)}, u32[]{:S(2)}, u32[]{:S(2)}) collective-permute-start(bf16[2,768,128]{2,1,0:T(8,128)(2,1)S(1)} %copy-done.7), channel_id=1, source_target_pairs={{0,24},{8,0},{16,8},{24,16},{1,25},{9,1},{17,9},{25,17},{2,26},{10... | collective-permute-start | bytes 1179656 | tf_op jit(solution)/shard_map/ppermute | solution.py:336
  25.1 17.1 %collective-permute-start.15 = (bf16[768,128]{1,0:T(8,128)(2,1)S(1)}, bf16[768,128]{1,0:T(8,128)(2,1)S(1)}, u32[]{:S(2)}, u32[]{:S(2)}) collective-permute-start(bf16[768,128]{1,0:T(8,128)(2,1)S(1)} %collective-permute-done.8.refs_11_), channel_id=1, source_target_pairs={{0,8},{8,16},{16,24},{24,0},{1,9},{9,17},{17,25},{25,1},{2,10},{10... | collective-permute-start | bytes 589832 | tf_op jit(solution)/shard_map/ppermute | solution.py:339
  28.1 14.1 %collective-permute-start.16 = (bf16[768,128]{1,0:T(8,128)(2,1)S(1)}, bf16[768,128]{1,0:T(8,128)(2,1)S(1)}, u32[]{:S(2)}, u32[]{:S(2)}) collective-permute-start(bf16[768,128]{1,0:T(8,128)(2,1)S(1)} %collective-permute-done.8.refs_11_), channel_id=1, source_target_pairs={{0,24},{8,0},{16,8},{24,16},{1,25},{9,1},{17,9},{25,17},{2,26},{10... | collective-permute-start | bytes 589832 | tf_op jit(solution)/shard_map/ppermute | solution.py:339
  42.3 2.6 %collective-permute-start.22 = (f32[8,256]{1,0:T(8,128)S(1)}, f32[8,256]{1,0:T(8,128)S(1)}, u32[]{:S(2)}, u32[]{:S(2)}) collective-permute-start(f32[8,256]{1,0:T(8,128)S(1)} %get-tuple-element.41), channel_id=1, source_target_pairs={{0,32},{32,0},{64,96},{96,64},{1,33},{33,1},{65,97},{97,65},{2,34}... | collective-permute-start | bytes 24584 | tf_op jit(solution)/shard_map/ppermute | solution.py:239
  42.4 6.5 %collective-permute-start.23 = (f32[8,256]{1,0:T(8,128)S(1)}, f32[8,256]{1,0:T(8,128)S(1)}, u32[]{:S(2)}, u32[]{:S(2)}) collective-permute-start(f32[8,256]{1,0:T(8,128)S(1)} %get-tuple-element.41), channel_id=1, source_target_pairs={{0,0},{32,64},{64,32},{96,96},{1,1},{33,65},{65,33},{97,97},{2,2},... | collective-permute-start | bytes 24584 | tf_op jit(solution)/shard_map/ppermute | solution.py:239
  44.3 11.8 %collective-permute-start.17 = (bf16[2,768,128]{2,1,0:T(8,128)(2,1)S(1)}, bf16[2,768,128]{2,1,0:T(8,128)(2,1)S(1)}, u32[]{:S(2)}, u32[]{:S(2)}) collective-permute-start(bf16[2,768,128]{2,1,0:T(8,128)(2,1)S(1)} %collective-permute-done.13.refs_5_), channel_id=1, source_target_pairs={{0,32},{32,0},{64,96},{96,64},{1,33},{33,1},{65,97},{97,65},{2,34}... | collective-permute-start | bytes 1179656 | tf_op jit(solution)/shard_map/ppermute | solution.py:346
  44.4 11.7 %collective-permute-start.18 = (bf16[2,768,128]{2,1,0:T(8,128)(2,1)S(1)}, bf16[2,768,128]{2,1,0:T(8,128)(2,1)S(1)}, u32[]{:S(2)}, u32[]{:S(2)}) collective-permute-start(bf16[2,768,128]{2,1,0:T(8,128)(2,1)S(1)} %collective-permute-done.14.refs_6_), channel_id=1, source_target_pairs={{0,32},{32,0},{64,96},{96,64},{1,33},{33,1},{65,97},{97,65},{2,34}... | collective-permute-start | bytes 1179656 | tf_op jit(solution)/shard_map/ppermute | solution.py:346
  48.9 3.8 %collective-permute-start.24 = (f32[24,256]{1,0:T(8,128)S(1)}, f32[24,256]{1,0:T(8,128)S(1)}, u32[]{:S(2)}, u32[]{:S(2)}) collective-permute-start(f32[24,256]{1,0:T(8,128)S(1)} %constant_dynamic-update-slice_fusion.refs_16_), channel_id=1, source_target_pairs={{0,8},{8,16},{16,24},{24,0},{1,9},{9,17},{17,25},{25,1},{2,10},{10... | collective-permute-start | bytes 73736 | tf_op jit(solution)/shard_map/ppermute | solution.py:240
  50.8 3.8 %collective-permute-start.25 = (f32[24,256]{1,0:T(8,128)S(1)}, f32[24,256]{1,0:T(8,128)S(1)}, u32[]{:S(2)}, u32[]{:S(2)}) collective-permute-start(f32[24,256]{1,0:T(8,128)S(1)} %constant_dynamic-update-slice_fusion.refs_16_), channel_id=1, source_target_pairs={{0,24},{8,0},{16,8},{24,16},{1,25},{9,1},{17,9},{25,17},{2,26},{10... | collective-permute-start | bytes 73736 | tf_op jit(solution)/shard_map/ppermute | solution.py:240
  50.9 3.7 %collective-permute-start.19 = (bf16[768,128]{1,0:T(8,128)(2,1)S(1)}, bf16[768,128]{1,0:T(8,128)(2,1)S(1)}, u32[]{:S(2)}, u32[]{:S(2)}) collective-permute-start(bf16[768,128]{1,0:T(8,128)(2,1)S(1)} %collective-permute-done.8.refs_11_), channel_id=1, source_target_pairs={{0,32},{32,0},{64,96},{96,64},{1,33},{33,1},{65,97},{97,65},{2,34}... | collective-permute-start | bytes 589832 | tf_op jit(solution)/shard_map/ppermute | solution.py:347
  (20 other events, 234.1 us)
where the time goes:
time: 72.7 us; the launch traced here: 71.4 us
  Pallas kernels  30.6 us (42%)
  waiting for transfers between devices  19 us (26%)
  starting transfers between devices  18.8 us (26%)
  other arithmetic  1.13 us (2%)
  between operations  0.97 us (1%)
  local copies, waits for them, and re-layouts  0.92 us (1%)
    pallas_call x1, Pallas kernels, key_call(): pl.pallas_call(lambda *refs: key_kernel(columns, tile, scale, *refs), out...  14.5 us
    pallas_call x1, Pallas kernels, query_call(): pl.pallas_call(lambda *refs: query_kernel(columns, tile, scale, *refs), o...  14 us
    ppermute x2, waiting for transfers between devices, body(): kv_up, kv_down = (send(kv, ROWS, before), send(kv, ROWS, after))  4.4 us
    ppermute x1, waiting for transfers between devices, spread_small(): lax.ppermute(x, TM, far)  3.95 us
    ppermute x2, waiting for transfers between devices, body(): half_up, half_down = (send(half, ROWS, before), send(half, ROWS, after))  3.49 us
    ppermute x1, starting transfers between devices, body(): qg_half = send(jnp.where(inner, qg[0], qg_o[1]), TM, ring(TM, 2))  3.06 us
    ppermute x1, starting transfers between devices, body(): send(qg_half, ROWS, before)  3.02 us
    ppermute x2, starting transfers between devices, body(): qg_up, qg_down = (send(qg_next, ROWS, before), send(qg_next, ROWS, after))  2.33 us
  transfers between devices with their start and end apart: 26, of which 9 were waited for; matrix products, arithmetic and copies ran while one was open for 2% of the time, Pallas kernels for 20%

commit v1 on v0

--- a/solution.py
+++ b/solution.py
@@ -12,8 +12,8 @@
 SLOTS = 9
 ROOM = 32
 GROUP = 12
-LIST = 28
-BIG = 6
+SUB = 3
+TURN = 3
 ROW_STEPS = (0, -1, 1)
 NT = (((1,), (1,)), ((), ()))
 NN = (((1,), (0,)), ((), ()))
@@ -38,28 +38,46 @@
     lists[list_size(columns) - 1] = (n + GROUP - 1) // GROUP
 
 
-def find_column_pairs(mask, lists, columns):
+def list_size(columns):
+    return 27 * columns + GROUP
+
+
+def find_subgroups(mask, lists, columns):
     near = 1 - 2 * lax.rem(lax.axis_index(TM), 2)
     frame_steps = (0, near, -near)
+    n = jnp.int32(0)
     for c in range(columns):
-        n = jnp.int32(0)
         for slot in range(SLOTS):
             dt, dr = frame_steps[slot // 3], ROW_STEPS[slot % 3]
             for other in range(max(c - 1, 0), min(c + 2, columns)):
-                lists[c * LIST + n] = slot * columns + other
+                lists[n] = slot * columns + other
                 n = n + mask[0, 0, c, 0, 9 * (dt + 1) + 3 * (dr + 1) + other - c + 1]
-        lists[c * LIST + n] = c
-        lists[columns * LIST + c] = n
-
-
-def list_size(columns):
-    return 27 * columns + GROUP
-
-
-def pack_kernel(columns, mask, q, k, v, g, kv, qg, pairs, column_pairs):
-    kv[0], kv[1], qg[0], qg[1] = k[...], v[...], q[...], g[...]
+        for extra in range(SUB - 1):
+            lists[n + extra] = SLOTS * columns
+        end = (n + SUB - 1) // SUB
+        lists[places(columns) - columns + c] = end
+        n = end * SUB
+    for extra in range(SUB * (TURN - 1)):
+        lists[n + extra] = SLOTS * columns
+
+
+def subgroups(columns):
+    most = sum(-(-9 * (min(c + 2, columns) - max(c - 1, 0)) // SUB) for c in range(columns))
+    return -(-most // TURN) * TURN
+
+
+def places(columns):
+    return (subgroups(columns) + TURN) * SUB + columns
+
+
+def pack_kv_kernel(k, v, kv):
+    kv[0], kv[1] = k[...], v[...]
+
+
+def pack_qg_kernel(columns, mask, q, g, qg, pairs, subgroup_pairs):
+    qg[0], qg[1] = q[...], g[...]
     find_pairs(mask, pairs, columns)
-    find_column_pairs(mask, column_pairs, columns)
+    find_subgroups(mask, subgroup_pairs, columns)
 
 
 def fetch(own, slots, near, mine, sems):
@@ -156,65 +174,61 @@
     grad_q[...] = (acc[:columns * tile, :] * low[:columns * tile, :]).astype(BF16)
 
 
-def grouped(n, run):
-    many = n // BIG
-
-    def big(i, carry):
-        run(BIG * i, BIG)
+def for_turns(columns, lists, run):
+    ends = [lists[places(columns) - columns + c] for c in range(columns)]
+
+    def step(i, carry):
+        subs = []
+        for j in range(TURN):
+            at = TURN * i + j
+            column = sum([(at >= end).astype(jnp.int32) for end in ends[:-1]], jnp.int32(0))
+            subs.append((column, [lists[SUB * at + p] for p in range(SUB)]))
+        run(i, subs)
         return carry
 
-    def small(i, carry):
-        run(BIG * many + 2 * i, 2)
-        return carry
-
-    lax.fori_loop(0, many, big, 0)
-    lax.fori_loop(0, (n - BIG * many + 1) // 2, small, 0)
+    lax.fori_loop(0, (ends[-1] + TURN - 1) // TURN, step, 0)
 
 
 def key_kernel(columns, tile, scale, lists, *refs):
     own, slots, sets = refs[:4], refs[4:SLOTS + 6], refs[SLOTS + 6:SLOTS + 9]
-    grad_k, grad_v, near, mine, logs, deltas, k_acc, v_acc, sems = refs[SLOTS + 9:]
+    grad_k, grad_v, near, mine, logs, deltas, k_acc, v_acc, sems = refs[SLOTS + 9:SLOTS + 18]
+    probs, scores = refs[SLOTS + 18:SLOTS + 18 + TURN], refs[SLOTS + 18 + TURN:]
     copies = fetch(own, slots, near, mine, sems)
+    spare = pl.ds(SLOTS * columns * tile, tile)
+    near[:, spare] = jnp.zeros((2, tile, near.shape[2]), BF16)
     for slot in range(SLOTS):
         first = 8 * (slot // 3)
         logs[slot * columns:(slot + 1) * columns, :] = sets[slot % 3][first:first + columns, :]
         deltas[slot * columns:(slot + 1) * columns, :] = sets[slot % 3][first + 4:first + 4 + columns, :]
     logs[SLOTS * columns:, :] = jnp.full((5, tile), 1e30, F32)
+    deltas[SLOTS * columns:, :] = jnp.zeros((5, tile), F32)
+    k_acc[...] = jnp.zeros(k_acc.shape, F32)
+    v_acc[...] = jnp.zeros(v_acc.shape, F32)
     for copy in copies:
         copy.wait()
     unit = scale * math.log2(math.e)
 
-    def one_column(c, carry):
-        rows = pl.ds(pl.multiple_of(c * tile, tile), tile)
-        n = lists[columns * LIST + c]
-        k_acc[...] = jnp.zeros(k_acc.shape, F32)
-        v_acc[...] = jnp.zeros(v_acc.shape, F32)
-
-        def step(first, size):
-            k = mine[0, rows, :]
-            v = mine[1, rows, :]
-            sum_v = v_acc[...]
-            sum_k = k_acc[...]
-            for j in range(size):
-                t = lists[c * LIST + first + j]
-                at = pl.ds(pl.multiple_of(t * tile, tile), tile)
-                q, g = near[0, at, :], near[1, at, :]
-                held = jnp.where(first + j < n, t, SLOTS * columns) if size == 2 and j == 1 else t
-                log_total = logs[pl.ds(held, 1), :]
-                delta = deltas[pl.ds(t, 1), :]
-                p = jnp.exp2(dot(k, q, NT) * unit - log_total)
-                sum_v = sum_v + dot(p.astype(BF16), g, NN)
-                ds = p * (dot(v, g, NT) - delta)
-                sum_k = sum_k + dot(ds.astype(BF16), q, NN)
-            v_acc[...] = sum_v
-            k_acc[...] = sum_k
-
-        grouped(n, step)
-        grad_k[rows, :] = (k_acc[...] * scale).astype(BF16)
-        grad_v[rows, :] = v_acc[...].astype(BF16)
-        return carry
-
-    lax.fori_loop(0, columns, one_column, 0)
+    def rows(index):
+        return pl.ds(pl.multiple_of(index * tile, tile), tile)
+
+    def stacked(which, tiles):
+        return jnp.concatenate([near[which, rows(t), :] for t in tiles], 0)
+
+    def step(i, subs):
+        for j, (c, tiles) in enumerate(subs):
+            k, v = mine[0, rows(c), :], mine[1, rows(c), :]
+            for n, t in enumerate(tiles):
+                part = slice(n * tile, (n + 1) * tile)
+                p = jnp.exp2(dot(k, near[0, rows(t), :], NT) * unit - logs[pl.ds(t, 1), :])
+                probs[j][:, part] = p.astype(BF16)
+                w = dot(v, near[1, rows(t), :], NT) - deltas[pl.ds(t, 1), :]
+                scores[j][:, part] = (p * w).astype(BF16)
+            v_acc[rows(c), :] += dot(probs[j][...], stacked(1, tiles), NN)
+            k_acc[rows(c), :] += dot(scores[j][...], stacked(0, tiles), NN)
+
+    for_turns(columns, lists, step)
+    grad_k[...] = (k_acc[...] * scale).astype(BF16)
+    grad_v[...] = v_acc[...].astype(BF16)
 
 
 def ring(axis, step):
@@ -281,18 +295,19 @@
     tokens, width = q.shape
     tile = tokens // columns
     field = jax.ShapeDtypeStruct((tokens, width), BF16)
-    total = pltpu.VMEM((tile, width), F32)
+    total = pltpu.VMEM((tokens, width), F32)
     return pl.pallas_call(
         lambda *refs: key_kernel(columns, tile, scale, *refs),
         out_shape=(field, field),
         in_specs=[SMEM] + [HBM] * 4 + [ANY] * (SLOTS + 2) + [VMEM] * 3,
         out_specs=(VMEM, VMEM),
         scratch_shapes=[
-            pltpu.VMEM((2, SLOTS * tokens, width), BF16),
-            pltpu.VMEM((2, tokens + tile, width), BF16),
+            pltpu.VMEM((2, SLOTS * tokens + tile, width), BF16),
+            pltpu.VMEM((2, tokens, width), BF16),
             *[pltpu.VMEM((SLOTS * columns + 5, tile), F32)] * 2,
             total, total,
             pltpu.SemaphoreType.DMA((SLOTS + 6,)),
+            *[pltpu.VMEM((tile, SUB * tile), BF16)] * (2 * TURN),
         ],
         compiler_params=PARAMS,
         cost_estimate=pl.CostEstimate(
@@ -309,21 +324,24 @@
     flat = lambda x: x.reshape(tokens, width)
     pair = jax.ShapeDtypeStruct((2, tokens, width), BF16)
     own = [flat(x) for x in (queries, keys, values, d_out)]
-    kv, qg, pairs, column_pairs = pl.pallas_call(
-        lambda *refs: pack_kernel(columns, *refs),
-        out_shape=(
-            pair, pair,
-            jax.ShapeDtypeStruct((list_size(columns),), jnp.int32),
-            jax.ShapeDtypeStruct((columns * (LIST + 1),), jnp.int32),
-        ),
-        in_specs=[SMEM] + [VMEM] * 4,
-        out_specs=(VMEM, VMEM, SMEM, SMEM),
-        name="pack",
-    )(window_mask, *own)
+    q, k, v, g = own
+    kv = pl.pallas_call(pack_kv_kernel, out_shape=pair, in_specs=[VMEM] * 2, out_specs=VMEM, name="pack_kv")(k, v)
     before, after, near, far = moves()
     send = lax.ppermute
     kv_o = send(kv, TM, near)
     kv_up, kv_down = send(kv, ROWS, before), send(kv, ROWS, after)
+    kv_o, q, g = then(kv_o, q, g)
+    qg, pairs, subgroup_pairs = pl.pallas_call(
+        lambda *refs: pack_qg_kernel(columns, *refs),
+        out_shape=(
+            pair,
+            jax.ShapeDtypeStruct((list_size(columns),), jnp.int32),
+            jax.ShapeDtypeStruct((places(columns),), jnp.int32),
+        ),
+        in_specs=[SMEM] + [VMEM] * 2,
+        out_specs=(VMEM, SMEM, SMEM),
+        name="pack_qg",
+    )(window_mask, q, g)
     frame = lax.axis_index(TM)
     inner = (frame > 0) & (frame < lax.axis_size(TM) - 1)
     half = send(jnp.where(inner, kv[0], kv_o[1]), TM, ring(TM, 2))
@@ -348,7 +366,7 @@
     near_qg = [
         qg_up, qg_down, qg_o, qg_ou, qg_od, qg_rest, qg_half, qg_rest_up, qg_half_up, qg_rest_down, qg_half_down
     ]
-    grad_k, grad_v = key_call(columns, column_pairs, *own, near_qg, near_stats, scale)
+    grad_k, grad_v = key_call(columns, subgroup_pairs, *own, near_qg, near_stats, scale)
     return tuple(x.reshape(queries.shape) for x in (attended, grad_q, grad_k, grad_v))
 
 

time: 72.7 us -> 71.5 us (0.983)
  the two profiles are of different devices: /device:TPU:112 before, /device:TPU:11 now
where the time goes in v1:
time: 71.5 us; the launch traced here: 70.3 us
  Pallas kernels  29.6 us (41%)
  starting transfers between devices  24.2 us (34%)
  waiting for transfers between devices  14.6 us (20%)
  local copies, waits for them, and re-layouts  0.92 us (1%)
  between operations  0.92 us (1%)
    pallas_call x1, Pallas kernels, query_call(): pl.pallas_call(lambda *refs: query_kernel(columns, tile, scale, *refs), o...  14 us
    pallas_call x1, Pallas kernels, key_call(): pl.pallas_call(lambda *refs: key_kernel(columns, tile, scale, *refs), out...  11.9 us
    ppermute x2, waiting for transfers between devices, body(): kv_up, kv_down = (send(kv, ROWS, before), send(kv, ROWS, after))  3.81 us
    ppermute x1, starting transfers between devices, body(): half = send(jnp.where(inner, kv[0], kv_o[1]), TM, ring(TM, 2))  3.68 us
    ppermute x1, waiting for transfers between devices, spread_small(): lax.ppermute(x, TM, far)  3.32 us
    ppermute x2, starting transfers between devices, body(): kv_ou, kv_od = (send(kv_up, TM, near), send(kv_down, TM, near))  2.93 us
    ppermute x1, starting transfers between devices, body(): qg_half = send(jnp.where(inner, qg[0], qg_o[1]), TM, ring(TM, 2))  2.8 us
    ppermute x1, starting transfers between devices, spread_small(): lax.ppermute(x, TM, far)  2.55 us
  transfers between devices with their start and end apart: 26, of which 11 were waited for; matrix products, arithmetic and copies ran while one was open for 0% of the time, Pallas kernels for 23%

profile of v1, /device:TPU:11, one launch (start us, length us, event | category | flops | bytes accessed | tf_op | source)
XLA Modules:
  0.0 70.3 jit_solution(16165294358047777813)
XLA Ops:
  0.6 1.8 %pack_kv.1 = bf16[2,768,128]{2,1,0:T(8,128)(2,1)} custom-call(bf16[768,128]{1,0:T(8,128)(2,1)} %bitcast.26, bf16[768,128]{1,0:T(8,128)(2,1)} %bitcast.29), custom_call_target="tpu_custom_call" | custom-call | tf_op jit(solution)/shard_map/pack_kv/pallas_call | solution.py:328
  3.1 1.3 %collective-permute-start.1 = (bf16[2,768,128]{2,1,0:T(8,128)(2,1)}, bf16[2,768,128]{2,1,0:T(8,128)(2,1)S(1)}, u32[]{:S(2)}, u32[]{:S(2)}) collective-permute-start(bf16[2,768,128]{2,1,0:T(8,128)(2,1)} %pack_kv.1), channel_id=1, source_target_pairs={{0,8},{8,16},{16,24},{24,0},{1,9},{9,17},{17,25},{25,1},{2,10},{10... | collective-permute-start | bytes 1179656 | tf_op jit(solution)/shard_map/ppermute | solution.py:332
  4.7 2.0 %pack_qg.1 = (bf16[2,768,128]{2,1,0:T(8,128)(2,1)}, s32[93]{0:T(128)}, s32[75]{0:T(128)}) custom-call(s32[1,1,3,1,27]{4,3,2,1,0:T(1,128)} %refs_0_.1, bf16[768,128]{1,0:T(8,128)(2,1)} %bitcast.20, bf16[768,128]{1,0:T(8,128)(2,1)} %bitcast.23), custom_call_target="tpu_custom_call" | custom-call | tf_op jit(solution)/shard_map/pack_qg/pallas_call | solution.py:334
  7.2 3.7 %collective-permute-start.5 = (bf16[768,128]{1,0:T(8,128)(2,1)S(1)}, bf16[768,128]{1,0:T(8,128)(2,1)S(1)}, u32[]{:S(2)}, u32[]{:S(2)}) collective-permute-start(bf16[768,128]{1,0:T(8,128)(2,1)S(1)} %fusion.1), channel_id=1, source_target_pairs={{0,64},{32,96},{64,0},{96,32},{1,65},{33,97},{65,1},{97,33},{2,66}... | collective-permute-start | bytes 589832 | tf_op jit(solution)/shard_map/ppermute | solution.py:347
  11.0 3.0 %collective-permute-done.1.refs_5_ = bf16[2,768,128]{2,1,0:T(8,128)(2,1)S(1)} collective-permute-done((bf16[2,768,128]{2,1,0:T(8,128)(2,1)}, bf16[2,768,128]{2,1,0:T(8,128)(2,1)S(1)}, u32[]{:S(2)}, u32[]{:S(2)}) %collective-permute-start.1) | collective-permute-done | bytes 393248 | tf_op jit(solution)/shard_map/ppermute | solution.py:332
  14.1 0.8 %collective-permute-start.3 = (bf16[2,768,128]{2,1,0:T(8,128)(2,1)S(1)}, bf16[2,768,128]{2,1,0:T(8,128)(2,1)S(1)}, u32[]{:S(2)}, u32[]{:S(2)}) collective-permute-start(bf16[2,768,128]{2,1,0:T(8,128)(2,1)S(1)} %collective-permute-done.1.refs_5_), channel_id=1, source_target_pairs={{0,32},{32,0},{64,96},{96,64},{1,33},{33,1},{65,97},{97,65},{2,34}... | collective-permute-start | bytes 1179656 | tf_op jit(solution)/shard_map/ppermute | solution.py:353
  14.8 1.2 %collective-permute-done.5.refs_11_ = bf16[768,128]{1,0:T(8,128)(2,1)S(1)} collective-permute-done((bf16[768,128]{1,0:T(8,128)(2,1)S(1)}, bf16[768,128]{1,0:T(8,128)(2,1)S(1)}, u32[]{:S(2)}, u32[]{:S(2)}) %collective-permute-start.5) | collective-permute-done | bytes 196640 | tf_op jit(solution)/shard_map/ppermute | solution.py:347
  16.3 1.2 %collective-permute-start.9 = (bf16[768,128]{1,0:T(8,128)(2,1)S(1)}, bf16[768,128]{1,0:T(8,128)(2,1)S(1)}, u32[]{:S(2)}, u32[]{:S(2)}) collective-permute-start(bf16[768,128]{1,0:T(8,128)(2,1)S(1)} %collective-permute-done.5.refs_11_), channel_id=1, source_target_pairs={{0,8},{8,16},{16,24},{24,0},{1,9},{9,17},{17,25},{25,1},{2,10},{10... | collective-permute-start | bytes 589832 | tf_op jit(solution)/shard_map/ppermute | solution.py:351
  17.5 2.8 %collective-permute-start.8 = (bf16[768,128]{1,0:T(8,128)(2,1)S(1)}, bf16[768,128]{1,0:T(8,128)(2,1)S(1)}, u32[]{:S(2)}, u32[]{:S(2)}) collective-permute-start(bf16[768,128]{1,0:T(8,128)(2,1)S(1)} %fusion), channel_id=1, source_target_pairs={{0,64},{32,96},{64,0},{96,32},{1,65},{33,97},{65,1},{97,33},{2,66}... | collective-permute-start | bytes 589832 | tf_op jit(solution)/shard_map/ppermute | solution.py:349
  20.3 0.8 %collective-permute-done.2.refs_6_ = bf16[2,768,128]{2,1,0:T(8,128)(2,1)S(1)} collective-permute-done((bf16[2,768,128]{2,1,0:T(8,128)(2,1)S(1)}, bf16[2,768,128]{2,1,0:T(8,128)(2,1)S(1)}, u32[]{:S(2)}, u32[]{:S(2)}) %collective-permute-start.2) | collective-permute-done | bytes 393248 | tf_op jit(solution)/shard_map/ppermute | solution.py:332
  21.1 2.1 %collective-permute-start.4 = (bf16[2,768,128]{2,1,0:T(8,128)(2,1)S(1)}, bf16[2,768,128]{2,1,0:T(8,128)(2,1)S(1)}, u32[]{:S(2)}, u32[]{:S(2)}) collective-permute-start(bf16[2,768,128]{2,1,0:T(8,128)(2,1)S(1)} %collective-permute-done.2.refs_6_), channel_id=1, source_target_pairs={{0,32},{32,0},{64,96},{96,64},{1,33},{33,1},{65,97},{97,65},{2,34}... | collective-permute-start | bytes 1179656 | tf_op jit(solution)/shard_map/ppermute | solution.py:353
  23.3 2.1 %collective-permute-done.10.refs_15_ = bf16[768,128]{1,0:T(8,128)(2,1)S(1)} collective-permute-done((bf16[768,128]{1,0:T(8,128)(2,1)S(1)}, bf16[768,128]{1,0:T(8,128)(2,1)S(1)}, u32[]{:S(2)}, u32[]{:S(2)}) %collective-permute-start.10) | collective-permute-done | bytes 196640 | tf_op jit(solution)/shard_map/ppermute | solution.py:351
  25.3 1.3 %collective-permute-start.6 = (bf16[768,128]{1,0:T(8,128)(2,1)S(1)}, bf16[768,128]{1,0:T(8,128)(2,1)S(1)}, u32[]{:S(2)}, u32[]{:S(2)}) collective-permute-start(bf16[768,128]{1,0:T(8,128)(2,1)S(1)} %collective-permute-done.5.refs_11_), channel_id=1, source_target_pairs={{0,32},{32,0},{64,96},{96,64},{1,33},{33,1},{65,97},{97,65},{2,34}... | collective-permute-start | bytes 589832 | tf_op jit(solution)/shard_map/ppermute | solution.py:352
  27.7 1.3 %collective-permute-start.13 = (bf16[2,768,128]{2,1,0:T(8,128)(2,1)S(1)}, bf16[2,768,128]{2,1,0:T(8,128)(2,1)S(1)}, u32[]{:S(2)}, u32[]{:S(2)}) collective-permute-start(bf16[2,768,128]{2,1,0:T(8,128)(2,1)S(1)} %copy-done.9), channel_id=1, source_target_pairs={{0,8},{8,16},{16,24},{24,0},{1,9},{9,17},{17,25},{25,1},{2,10},{10... | collective-permute-start | bytes 1179656 | tf_op jit(solution)/shard_map/ppermute | solution.py:354
  29.2 2.1 %collective-permute-start.15 = (bf16[768,128]{1,0:T(8,128)(2,1)S(1)}, bf16[768,128]{1,0:T(8,128)(2,1)S(1)}, u32[]{:S(2)}, u32[]{:S(2)}) collective-permute-start(bf16[768,128]{1,0:T(8,128)(2,1)S(1)} %collective-permute-done.8.refs_11_), channel_id=1, source_target_pairs={{0,8},{8,16},{16,24},{24,0},{1,9},{9,17},{17,25},{25,1},{2,10},{10... | collective-permute-start | bytes 589832 | tf_op jit(solution)/shard_map/ppermute | solution.py:357
  32.0 14.0 %query_side.1 = (bf16[768,128]{1,0:T(8,128)(2,1)}, bf16[768,128]{1,0:T(8,128)(2,1)}, f32[8,256]{1,0:T(8,128)S(1)}) custom-call(s32[93]{0:T(128)S(1)} %copy-done.5, bf16[768,128]{1,0:T(8,128)(2,1)S(1)} %bitcast.27, bf16[768,128]{1,0:T(8,128)(2,1)S(1)} %bitcast.30, bf16[768,128]{1,0:T(8,128)(2,1)S(1)} %bitcast.21, bf16[768,128]{1,0:T(8,128)(2,1)S(1)} %bitcast.24, ...), custom_call_target="tpu_custom_call" | custom-call | flops 2684354560 | bytes 786432 | tf_op jit(solution)/shard_map/query_side/pallas_call | solution.py:274
  46.2 2.6 %collective-permute-start.23 = (f32[8,256]{1,0:T(8,128)S(1)}, f32[8,256]{1,0:T(8,128)S(1)}, u32[]{:S(2)}, u32[]{:S(2)}) collective-permute-start(f32[8,256]{1,0:T(8,128)S(1)} %get-tuple-element.45), channel_id=1, source_target_pairs={{0,0},{32,64},{64,32},{96,96},{1,1},{33,65},{65,33},{97,97},{2,2},... | collective-permute-start | bytes 24584 | tf_op jit(solution)/shard_map/ppermute | solution.py:253
  49.4 3.3 %collective-permute-done.23 = f32[8,256]{1,0:T(8,128)S(1)} collective-permute-done((f32[8,256]{1,0:T(8,128)S(1)}, f32[8,256]{1,0:T(8,128)S(1)}, u32[]{:S(2)}, u32[]{:S(2)}) %collective-permute-start.23) | collective-permute-done | bytes 8224 | tf_op jit(solution)/shard_map/ppermute | solution.py:253
  52.7 0.7 %collective-permute-start.24 = (f32[24,256]{1,0:T(8,128)S(1)}, f32[24,256]{1,0:T(8,128)S(1)}, u32[]{:S(2)}, u32[]{:S(2)}) collective-permute-start(f32[24,256]{1,0:T(8,128)S(1)} %constant_dynamic-update-slice_fusion.refs_16_), channel_id=1, source_target_pairs={{0,8},{8,16},{16,24},{24,0},{1,9},{9,17},{17,25},{25,1},{2,10},{10... | collective-permute-start | bytes 73736 | tf_op jit(solution)/shard_map/ppermute | solution.py:254
  53.4 0.7 %collective-permute-start.25 = (f32[24,256]{1,0:T(8,128)S(1)}, f32[24,256]{1,0:T(8,128)S(1)}, u32[]{:S(2)}, u32[]{:S(2)}) collective-permute-start(f32[24,256]{1,0:T(8,128)S(1)} %constant_dynamic-update-slice_fusion.refs_16_), channel_id=1, source_target_pairs={{0,24},{8,0},{16,8},{24,16},{1,25},{9,1},{17,9},{25,17},{2,26},{10... | collective-permute-start | bytes 73736 | tf_op jit(solution)/shard_map/ppermute | solution.py:254
  54.1 1.2 %collective-permute-done.24.refs_17_ = f32[24,256]{1,0:T(8,128)S(1)} collective-permute-done((f32[24,256]{1,0:T(8,128)S(1)}, f32[24,256]{1,0:T(8,128)S(1)}, u32[]{:S(2)}, u32[]{:S(2)}) %collective-permute-start.24) | collective-permute-done | bytes 24608 | tf_op jit(solution)/shard_map/ppermute | solution.py:254
  55.4 0.7 %collective-permute-done.25.refs_18_ = f32[24,256]{1,0:T(8,128)S(1)} collective-permute-done((f32[24,256]{1,0:T(8,128)S(1)}, f32[24,256]{1,0:T(8,128)S(1)}, u32[]{:S(2)}, u32[]{:S(2)}) %collective-permute-start.25) | collective-permute-done | bytes 24608 | tf_op jit(solution)/shard_map/ppermute | solution.py:254
  56.8 0.7 %collective-permute-done.21.refs_14_ = bf16[768,128]{1,0:T(8,128)(2,1)S(1)} collective-permute-done((bf16[768,128]{1,0:T(8,128)(2,1)S(1)}, bf16[768,128]{1,0:T(8,128)(2,1)S(1)}, u32[]{:S(2)}, u32[]{:S(2)}) %collective-permute-start.21) | collective-permute-done | bytes 196640 | tf_op jit(solution)/shard_map/ppermute | solution.py:365
  58.4 11.9 %key_side.1 = (bf16[768,128]{1,0:T(8,128)(2,1)}, bf16[768,128]{1,0:T(8,128)(2,1)}) custom-call(s32[75]{0:T(128)S(1)} %copy-done.4, bf16[768,128]{1,0:T(8,128)(2,1)S(1)} %bitcast.22, bf16[768,128]{1,0:T(8,128)(2,1)S(1)} %bitcast.25, bf16[768,128]{1,0:T(8,128)(2,1)S(1)} %bitcast.28, bf16[768,128]{1,0:T(8,128)(2,1)S(1)} %bitcast.31, ...), custom_call_target="tpu_custom_call" | custom-call | flops 2147483648 | bytes 786432 | tf_op jit(solution)/shard_map/key_side/pallas_call | solution.py:299
  (75 shorter events, 6.1 us)
Async XLA Ops:
  2.4 2.2 %collective-permute-start = (bf16[2,768,128]{2,1,0:T(8,128)(2,1)}, bf16[2,768,128]{2,1,0:T(8,128)(2,1)S(1)}, u32[]{:S(2)}, u32[]{:S(2)}) collective-permute-start(bf16[2,768,128]{2,1,0:T(8,128)(2,1)} %pack_kv.1), channel_id=1, source_target_pairs={{0,32},{32,0},{64,96},{96,64},{1,33},{33,1},{65,97},{97,65},{2,34}... | collective-permute-start | bytes 1179656 | tf_op jit(solution)/shard_map/ppermute | solution.py:331
  3.1 11.0 %collective-permute-start.1 = (bf16[2,768,128]{2,1,0:T(8,128)(2,1)}, bf16[2,768,128]{2,1,0:T(8,128)(2,1)S(1)}, u32[]{:S(2)}, u32[]{:S(2)}) collective-permute-start(bf16[2,768,128]{2,1,0:T(8,128)(2,1)} %pack_kv.1), channel_id=1, source_target_pairs={{0,8},{8,16},{16,24},{24,0},{1,9},{9,17},{17,25},{25,1},{2,10},{10... | collective-permute-start | bytes 1179656 | tf_op jit(solution)/shard_map/ppermute | solution.py:332
  6.7 10.8 %collective-permute-start.7 = (bf16[2,768,128]{2,1,0:T(8,128)(2,1)}, bf16[2,768,128]{2,1,0:T(8,128)(2,1)S(1)}, u32[]{:S(2)}, u32[]{:S(2)}) collective-permute-start(bf16[2,768,128]{2,1,0:T(8,128)(2,1)} %get-tuple-element.39), channel_id=1, source_target_pairs={{0,32},{32,0},{64,96},{96,64},{1,33},{33,1},{65,97},{97,65},{2,34}... | collective-permute-start | bytes 1179656 | tf_op jit(solution)/shard_map/ppermute | solution.py:348
  7.2 8.8 %collective-permute-start.5 = (bf16[768,128]{1,0:T(8,128)(2,1)S(1)}, bf16[768,128]{1,0:T(8,128)(2,1)S(1)}, u32[]{:S(2)}, u32[]{:S(2)}) collective-permute-start(bf16[768,128]{1,0:T(8,128)(2,1)S(1)} %fusion.1), channel_id=1, source_target_pairs={{0,64},{32,96},{64,0},{96,32},{1,65},{33,97},{65,1},{97,33},{2,66}... | collective-permute-start | bytes 589832 | tf_op jit(solution)/shard_map/ppermute | solution.py:347
  10.9 10.3 %collective-permute-start.2 = (bf16[2,768,128]{2,1,0:T(8,128)(2,1)S(1)}, bf16[2,768,128]{2,1,0:T(8,128)(2,1)S(1)}, u32[]{:S(2)}, u32[]{:S(2)}) collective-permute-start(bf16[2,768,128]{2,1,0:T(8,128)(2,1)S(1)} %copy-done.6), channel_id=1, source_target_pairs={{0,24},{8,0},{16,8},{24,16},{1,25},{9,1},{17,9},{25,17},{2,26},{10... | collective-permute-start | bytes 1179656 | tf_op jit(solution)/shard_map/ppermute | solution.py:332
  14.1 14.9 %collective-permute-start.3 = (bf16[2,768,128]{2,1,0:T(8,128)(2,1)S(1)}, bf16[2,768,128]{2,1,0:T(8,128)(2,1)S(1)}, u32[]{:S(2)}, u32[]{:S(2)}) collective-permute-start(bf16[2,768,128]{2,1,0:T(8,128)(2,1)S(1)} %collective-permute-done.1.refs_5_), channel_id=1, source_target_pairs={{0,32},{32,0},{64,96},{96,64},{1,33},{33,1},{65,97},{97,65},{2,34}... | collective-permute-start | bytes 1179656 | tf_op jit(solution)/shard_map/ppermute | solution.py:353
  16.0 9.3 %collective-permute-start.10 = (bf16[768,128]{1,0:T(8,128)(2,1)S(1)}, bf16[768,128]{1,0:T(8,128)(2,1)S(1)}, u32[]{:S(2)}, u32[]{:S(2)}) collective-permute-start(bf16[768,128]{1,0:T(8,128)(2,1)S(1)} %collective-permute-done.5.refs_11_), channel_id=1, source_target_pairs={{0,24},{8,0},{16,8},{24,16},{1,25},{9,1},{17,9},{25,17},{2,26},{10... | collective-permute-start | bytes 589832 | tf_op jit(solution)/shard_map/ppermute | solution.py:351
  16.3 10.3 %collective-permute-start.9 = (bf16[768,128]{1,0:T(8,128)(2,1)S(1)}, bf16[768,128]{1,0:T(8,128)(2,1)S(1)}, u32[]{:S(2)}, u32[]{:S(2)}) collective-permute-start(bf16[768,128]{1,0:T(8,128)(2,1)S(1)} %collective-permute-done.5.refs_11_), channel_id=1, source_target_pairs={{0,8},{8,16},{16,24},{24,0},{1,9},{9,17},{17,25},{25,1},{2,10},{10... | collective-permute-start | bytes 589832 | tf_op jit(solution)/shard_map/ppermute | solution.py:351
  17.5 9.1 %collective-permute-start.8 = (bf16[768,128]{1,0:T(8,128)(2,1)S(1)}, bf16[768,128]{1,0:T(8,128)(2,1)S(1)}, u32[]{:S(2)}, u32[]{:S(2)}) collective-permute-start(bf16[768,128]{1,0:T(8,128)(2,1)S(1)} %fusion), channel_id=1, source_target_pairs={{0,64},{32,96},{64,0},{96,32},{1,65},{33,97},{65,1},{97,33},{2,66}... | collective-permute-start | bytes 589832 | tf_op jit(solution)/shard_map/ppermute | solution.py:349
  21.1 8.0 %collective-permute-start.4 = (bf16[2,768,128]{2,1,0:T(8,128)(2,1)S(1)}, bf16[2,768,128]{2,1,0:T(8,128)(2,1)S(1)}, u32[]{:S(2)}, u32[]{:S(2)}) collective-permute-start(bf16[2,768,128]{2,1,0:T(8,128)(2,1)S(1)} %collective-permute-done.2.refs_6_), channel_id=1, source_target_pairs={{0,32},{32,0},{64,96},{96,64},{1,33},{33,1},{65,97},{97,65},{2,34}... | collective-permute-start | bytes 1179656 | tf_op jit(solution)/shard_map/ppermute | solution.py:353
  25.3 2.3 %collective-permute-start.6 = (bf16[768,128]{1,0:T(8,128)(2,1)S(1)}, bf16[768,128]{1,0:T(8,128)(2,1)S(1)}, u32[]{:S(2)}, u32[]{:S(2)}) collective-permute-start(bf16[768,128]{1,0:T(8,128)(2,1)S(1)} %collective-permute-done.5.refs_11_), channel_id=1, source_target_pairs={{0,32},{32,0},{64,96},{96,64},{1,33},{33,1},{65,97},{97,65},{2,34}... | collective-permute-start | bytes 589832 | tf_op jit(solution)/shard_map/ppermute | solution.py:352
  26.6 4.7 %collective-permute-start.11 = (bf16[768,128]{1,0:T(8,128)(2,1)S(1)}, bf16[768,128]{1,0:T(8,128)(2,1)S(1)}, u32[]{:S(2)}, u32[]{:S(2)}) collective-permute-start(bf16[768,128]{1,0:T(8,128)(2,1)S(1)} %collective-permute-done.9.refs_13_), channel_id=1, source_target_pairs={{0,32},{32,0},{64,96},{96,64},{1,33},{33,1},{65,97},{97,65},{2,34}... | collective-permute-start | bytes 589832 | tf_op jit(solution)/shard_map/ppermute | solution.py:356
  26.7 5.3 %collective-permute-start.12 = (bf16[768,128]{1,0:T(8,128)(2,1)S(1)}, bf16[768,128]{1,0:T(8,128)(2,1)S(1)}, u32[]{:S(2)}, u32[]{:S(2)}) collective-permute-start(bf16[768,128]{1,0:T(8,128)(2,1)S(1)} %collective-permute-done.10.refs_15_), channel_id=1, source_target_pairs={{0,32},{32,0},{64,96},{96,64},{1,33},{33,1},{65,97},{97,65},{2,34}... | collective-permute-start | bytes 589832 | tf_op jit(solution)/shard_map/ppermute | solution.py:356
  27.7 18.3 %collective-permute-start.13 = (bf16[2,768,128]{2,1,0:T(8,128)(2,1)S(1)}, bf16[2,768,128]{2,1,0:T(8,128)(2,1)S(1)}, u32[]{:S(2)}, u32[]{:S(2)}) collective-permute-start(bf16[2,768,128]{2,1,0:T(8,128)(2,1)S(1)} %copy-done.9), channel_id=1, source_target_pairs={{0,8},{8,16},{16,24},{24,0},{1,9},{9,17},{17,25},{25,1},{2,10},{10... | collective-permute-start | bytes 1179656 | tf_op jit(solution)/shard_map/ppermute | solution.py:354
  29.0 17.1 %collective-permute-start.14 = (bf16[2,768,128]{2,1,0:T(8,128)(2,1)S(1)}, bf16[2,768,128]{2,1,0:T(8,128)(2,1)S(1)}, u32[]{:S(2)}, u32[]{:S(2)}) collective-permute-start(bf16[2,768,128]{2,1,0:T(8,128)(2,1)S(1)} %copy-done.9), channel_id=1, source_target_pairs={{0,24},{8,0},{16,8},{24,16},{1,25},{9,1},{17,9},{25,17},{2,26},{10... | collective-permute-start | bytes 1179656 | tf_op jit(solution)/shard_map/ppermute | solution.py:354
  29.2 16.9 %collective-permute-start.15 = (bf16[768,128]{1,0:T(8,128)(2,1)S(1)}, bf16[768,128]{1,0:T(8,128)(2,1)S(1)}, u32[]{:S(2)}, u32[]{:S(2)}) collective-permute-start(bf16[768,128]{1,0:T(8,128)(2,1)S(1)} %collective-permute-done.8.refs_11_), channel_id=1, source_target_pairs={{0,8},{8,16},{16,24},{24,0},{1,9},{9,17},{17,25},{25,1},{2,10},{10... | collective-permute-start | bytes 589832 | tf_op jit(solution)/shard_map/ppermute | solution.py:357
  31.3 14.8 %collective-permute-start.16 = (bf16[768,128]{1,0:T(8,128)(2,1)S(1)}, bf16[768,128]{1,0:T(8,128)(2,1)S(1)}, u32[]{:S(2)}, u32[]{:S(2)}) collective-permute-start(bf16[768,128]{1,0:T(8,128)(2,1)S(1)} %collective-permute-done.8.refs_11_), channel_id=1, source_target_pairs={{0,24},{8,0},{16,8},{24,16},{1,25},{9,1},{17,9},{25,17},{2,26},{10... | collective-permute-start | bytes 589832 | tf_op jit(solution)/shard_map/ppermute | solution.py:357
  46.1 3.3 %collective-permute-start.22 = (f32[8,256]{1,0:T(8,128)S(1)}, f32[8,256]{1,0:T(8,128)S(1)}, u32[]{:S(2)}, u32[]{:S(2)}) collective-permute-start(f32[8,256]{1,0:T(8,128)S(1)} %get-tuple-element.45), channel_id=1, source_target_pairs={{0,32},{32,0},{64,96},{96,64},{1,33},{33,1},{65,97},{97,65},{2,34}... | collective-permute-start | bytes 24584 | tf_op jit(solution)/shard_map/ppermute | solution.py:253
  46.2 6.5 %collective-permute-start.23 = (f32[8,256]{1,0:T(8,128)S(1)}, f32[8,256]{1,0:T(8,128)S(1)}, u32[]{:S(2)}, u32[]{:S(2)}) collective-permute-start(f32[8,256]{1,0:T(8,128)S(1)} %get-tuple-element.45), channel_id=1, source_target_pairs={{0,0},{32,64},{64,32},{96,96},{1,1},{33,65},{65,33},{97,97},{2,2},... | collective-permute-start | bytes 24584 | tf_op jit(solution)/shard_map/ppermute | solution.py:253
  48.8 8.8 %collective-permute-start.17 = (bf16[2,768,128]{2,1,0:T(8,128)(2,1)S(1)}, bf16[2,768,128]{2,1,0:T(8,128)(2,1)S(1)}, u32[]{:S(2)}, u32[]{:S(2)}) collective-permute-start(bf16[2,768,128]{2,1,0:T(8,128)(2,1)S(1)} %collective-permute-done.13.refs_5_), channel_id=1, source_target_pairs={{0,32},{32,0},{64,96},{96,64},{1,33},{33,1},{65,97},{97,65},{2,34}... | collective-permute-start | bytes 1179656 | tf_op jit(solution)/shard_map/ppermute | solution.py:364
  48.8 8.7 %collective-permute-start.18 = (bf16[2,768,128]{2,1,0:T(8,128)(2,1)S(1)}, bf16[2,768,128]{2,1,0:T(8,128)(2,1)S(1)}, u32[]{:S(2)}, u32[]{:S(2)}) collective-permute-start(bf16[2,768,128]{2,1,0:T(8,128)(2,1)S(1)} %collective-permute-done.14.refs_6_), channel_id=1, source_target_pairs={{0,32},{32,0},{64,96},{96,64},{1,33},{33,1},{65,97},{97,65},{2,34}... | collective-permute-start | bytes 1179656 | tf_op jit(solution)/shard_map/ppermute | solution.py:364
  52.7 2.7 %collective-permute-start.24 = (f32[24,256]{1,0:T(8,128)S(1)}, f32[24,256]{1,0:T(8,128)S(1)}, u32[]{:S(2)}, u32[]{:S(2)}) collective-permute-start(f32[24,256]{1,0:T(8,128)S(1)} %constant_dynamic-update-slice_fusion.refs_16_), channel_id=1, source_target_pairs={{0,8},{8,16},{16,24},{24,0},{1,9},{9,17},{17,25},{25,1},{2,10},{10... | collective-permute-start | bytes 73736 | tf_op jit(solution)/shard_map/ppermute | solution.py:254
  53.4 2.7 %collective-permute-start.25 = (f32[24,256]{1,0:T(8,128)S(1)}, f32[24,256]{1,0:T(8,128)S(1)}, u32[]{:S(2)}, u32[]{:S(2)}) collective-permute-start(f32[24,256]{1,0:T(8,128)S(1)} %constant_dynamic-update-slice_fusion.refs_16_), channel_id=1, source_target_pairs={{0,24},{8,0},{16,8},{24,16},{1,25},{9,1},{17,9},{25,17},{2,26},{10... | collective-permute-start | bytes 73736 | tf_op jit(solution)/shard_map/ppermute | solution.py:254
  54.1 2.0 %collective-permute-start.19 = (bf16[768,128]{1,0:T(8,128)(2,1)S(1)}, bf16[768,128]{1,0:T(8,128)(2,1)S(1)}, u32[]{:S(2)}, u32[]{:S(2)}) collective-permute-start(bf16[768,128]{1,0:T(8,128)(2,1)S(1)} %collective-permute-done.8.refs_11_), channel_id=1, source_target_pairs={{0,32},{32,0},{64,96},{96,64},{1,33},{33,1},{65,97},{97,65},{2,34}... | collective-permute-start | bytes 589832 | tf_op jit(solution)/shard_map/ppermute | solution.py:365
  (21 other events, 239.9 us)

commit v2 on v1

--- a/solution.py
+++ b/solution.py
@@ -11,7 +11,7 @@
 F32, BF16 = jnp.float32, jnp.bfloat16
 SLOTS = 9
 ROOM = 32
-GROUP = 12
+GROUP = 14
 SUB = 3
 TURN = 3
 ROW_STEPS = (0, -1, 1)
@@ -70,12 +70,8 @@
     return (subgroups(columns) + TURN) * SUB + columns
 
 
-def pack_kv_kernel(k, v, kv):
-    kv[0], kv[1] = k[...], v[...]
-
-
-def pack_qg_kernel(columns, mask, q, g, qg, pairs, subgroup_pairs):
-    qg[0], qg[1] = q[...], g[...]
+def pack_kernel(columns, mask, q, k, v, g, kv, qg, pairs, subgroup_pairs):
+    kv[0], kv[1], qg[0], qg[1] = k[...], v[...], q[...], g[...]
     find_pairs(mask, pairs, columns)
     find_subgroups(mask, subgroup_pairs, columns)
 
@@ -324,24 +320,21 @@
     flat = lambda x: x.reshape(tokens, width)
     pair = jax.ShapeDtypeStruct((2, tokens, width), BF16)
     own = [flat(x) for x in (queries, keys, values, d_out)]
-    q, k, v, g = own
-    kv = pl.pallas_call(pack_kv_kernel, out_shape=pair, in_specs=[VMEM] * 2, out_specs=VMEM, name="pack_kv")(k, v)
+    kv, qg, pairs, subgroup_pairs = pl.pallas_call(
+        lambda *refs: pack_kernel(columns, *refs),
+        out_shape=(
+            pair, pair,
+            jax.ShapeDtypeStruct((list_size(columns),), jnp.int32),
+            jax.ShapeDtypeStruct((places(columns),), jnp.int32),
+        ),
+        in_specs=[SMEM] + [VMEM] * 4,
+        out_specs=(VMEM, VMEM, SMEM, SMEM),
+        name="pack",
+    )(window_mask, *own)
     before, after, near, far = moves()
     send = lax.ppermute
     kv_o = send(kv, TM, near)
     kv_up, kv_down = send(kv, ROWS, before), send(kv, ROWS, after)
-    kv_o, q, g = then(kv_o, q, g)
-    qg, pairs, subgroup_pairs = pl.pallas_call(
-        lambda *refs: pack_qg_kernel(columns, *refs),
-        out_shape=(
-            pair,
-            jax.ShapeDtypeStruct((list_size(columns),), jnp.int32),
-            jax.ShapeDtypeStruct((places(columns),), jnp.int32),
-        ),
-        in_specs=[SMEM] + [VMEM] * 2,
-        out_specs=(VMEM, SMEM, SMEM),
-        name="pack_qg",
-    )(window_mask, q, g)
     frame = lax.axis_index(TM)
     inner = (frame > 0) & (frame < lax.axis_size(TM) - 1)
     half = send(jnp.where(inner, kv[0], kv_o[1]), TM, ring(TM, 2))

time: 71.5 us -> 70.6 us (0.987)
  the two profiles are of different devices: /device:TPU:11 before, /device:TPU:17 now
where the time goes in v2:
time: 70.6 us; the launch traced here: 70.1 us
  starting transfers between devices  30 us (42%)
  Pallas kernels  26.7 us (38%)
  waiting for transfers between devices  10.5 us (15%)
  other arithmetic  1.13 us (2%)
  local copies, waits for them, and re-layouts  0.93 us (1%)
  between operations  0.9 us (1%)
    pallas_call x1, Pallas kernels, query_call(): pl.pallas_call(lambda *refs: query_kernel(columns, tile, scale, *refs), o...  12.7 us
    pallas_call x1, Pallas kernels, key_call(): pl.pallas_call(lambda *refs: key_kernel(columns, tile, scale, *refs), out...  11.9 us
    ppermute x1, starting transfers between devices, spread_small(): lax.ppermute(x, TM, far)  5.33 us
    ppermute x2, waiting for transfers between devices, body(): kv_up, kv_down = (send(kv, ROWS, before), send(kv, ROWS, after))  4.01 us
    ppermute x1, starting transfers between devices, body(): half = send(jnp.where(inner, kv[0], kv_o[1]), TM, ring(TM, 2))  3.68 us
    ppermute x2, starting transfers between devices, body(): kv_ou, kv_od = (send(kv_up, TM, near), send(kv_down, TM, near))  3.27 us
    ppermute x1, waiting for transfers between devices, spread_small(): lax.ppermute(frames, ROWS, after)  3.18 us
    ppermute x1, starting transfers between devices, body(): send(qg_half, ROWS, before)  2.83 us
  transfers between devices with their start and end apart: 26, of which 6 were waited for; matrix products, arithmetic and copies ran while one was open for 2% of the time, Pallas kernels for 18%

profile of v2, /device:TPU:17, one launch (start us, length us, event | category | flops | bytes accessed | tf_op | source)
XLA Modules:
  0.0 70.1 jit_solution(4807456440313145274)
XLA Ops:
  0.6 2.2 %pack.1 = (bf16[2,768,128]{2,1,0:T(8,128)(2,1)}, bf16[2,768,128]{2,1,0:T(8,128)(2,1)}, s32[95]{0:T(128)}, s32[75]{0:T(128)}) custom-call(s32[1,1,3,1,27]{4,3,2,1,0:T(1,128)} %refs_0_.1, bf16[768,128]{1,0:T(8,128)(2,1)} %bitcast.20, bf16[768,128]{1,0:T(8,128)(2,1)} %bitcast.23, bf16[768,128]{1,0:T(8,128)(2,1)} %bitcast.26, bf16[768,128]{1,0:T(8,128)(2,1)} %bitcast.29), custom_call_target="tpu_custom_call" | custom-call | tf_op jit(solution)/shard_map/pack/pallas_call | solution.py:323
  2.8 0.8 %collective-permute-start.2 = (bf16[2,768,128]{2,1,0:T(8,128)(2,1)}, bf16[2,768,128]{2,1,0:T(8,128)(2,1)S(1)}, u32[]{:S(2)}, u32[]{:S(2)}) collective-permute-start(bf16[2,768,128]{2,1,0:T(8,128)(2,1)} %get-tuple-element.25), channel_id=1, source_target_pairs={{0,32},{32,0},{64,96},{96,64},{1,33},{33,1},{65,97},{97,65},{2,34}... | collective-permute-start | bytes 1179656 | tf_op jit(solution)/shard_map/ppermute | solution.py:336
  3.7 1.0 %collective-permute-start = (bf16[2,768,128]{2,1,0:T(8,128)(2,1)}, bf16[2,768,128]{2,1,0:T(8,128)(2,1)S(1)}, u32[]{:S(2)}, u32[]{:S(2)}) collective-permute-start(bf16[2,768,128]{2,1,0:T(8,128)(2,1)} %get-tuple-element.25), channel_id=1, source_target_pairs={{0,8},{8,16},{16,24},{24,0},{1,9},{9,17},{17,25},{25,1},{2,10},{10... | collective-permute-start | bytes 1179656 | tf_op jit(solution)/shard_map/ppermute | solution.py:337
  5.1 1.1 %fusion.1 = bf16[768,128]{1,0:T(8,128)(2,1)S(1)} fusion(bf16[2,768,128]{2,1,0:T(8,128)(2,1)S(1)} %collective-permute-done.2.refs_7_, bf16[2,768,128]{2,1,0:T(8,128)(2,1)} %get-tuple-element.25, pred[]{:T(512)S(6)} %and.4), kind=kLoop, calls=%fused_computation.3 | loop fusion | flops 98304 | bytes 589825 | tf_op jit(solution)/shard_map/jit(_where)/select_n | solution.py:340
  6.3 3.7 %collective-permute-start.5 = (bf16[768,128]{1,0:T(8,128)(2,1)S(1)}, bf16[768,128]{1,0:T(8,128)(2,1)S(1)}, u32[]{:S(2)}, u32[]{:S(2)}) collective-permute-start(bf16[768,128]{1,0:T(8,128)(2,1)S(1)} %fusion.1), channel_id=1, source_target_pairs={{0,64},{32,96},{64,0},{96,32},{1,65},{33,97},{65,1},{97,33},{2,66}... | collective-permute-start | bytes 589832 | tf_op jit(solution)/shard_map/ppermute | solution.py:340
  10.1 4.0 %collective-permute-done.refs_5_ = bf16[2,768,128]{2,1,0:T(8,128)(2,1)S(1)} collective-permute-done((bf16[2,768,128]{2,1,0:T(8,128)(2,1)}, bf16[2,768,128]{2,1,0:T(8,128)(2,1)S(1)}, u32[]{:S(2)}, u32[]{:S(2)}) %collective-permute-start) | collective-permute-done | bytes 393248 | tf_op jit(solution)/shard_map/ppermute | solution.py:337
  14.1 1.3 %collective-permute-start.3 = (bf16[2,768,128]{2,1,0:T(8,128)(2,1)S(1)}, bf16[2,768,128]{2,1,0:T(8,128)(2,1)S(1)}, u32[]{:S(2)}, u32[]{:S(2)}) collective-permute-start(bf16[2,768,128]{2,1,0:T(8,128)(2,1)S(1)} %collective-permute-done.refs_5_), channel_id=1, source_target_pairs={{0,32},{32,0},{64,96},{96,64},{1,33},{33,1},{65,97},{97,65},{2,34}... | collective-permute-start | bytes 1179656 | tf_op jit(solution)/shard_map/ppermute | solution.py:346
  15.6 1.3 %collective-permute-start.9 = (bf16[768,128]{1,0:T(8,128)(2,1)S(1)}, bf16[768,128]{1,0:T(8,128)(2,1)S(1)}, u32[]{:S(2)}, u32[]{:S(2)}) collective-permute-start(bf16[768,128]{1,0:T(8,128)(2,1)S(1)} %collective-permute-done.5.refs_11_), channel_id=1, source_target_pairs={{0,8},{8,16},{16,24},{24,0},{1,9},{9,17},{17,25},{25,1},{2,10},{10... | collective-permute-start | bytes 589832 | tf_op jit(solution)/shard_map/ppermute | solution.py:344
  16.9 2.0 %collective-permute-start.4 = (bf16[2,768,128]{2,1,0:T(8,128)(2,1)S(1)}, bf16[2,768,128]{2,1,0:T(8,128)(2,1)S(1)}, u32[]{:S(2)}, u32[]{:S(2)}) collective-permute-start(bf16[2,768,128]{2,1,0:T(8,128)(2,1)S(1)} %collective-permute-done.1.refs_6_), channel_id=1, source_target_pairs={{0,32},{32,0},{64,96},{96,64},{1,33},{33,1},{65,97},{97,65},{2,34}... | collective-permute-start | bytes 1179656 | tf_op jit(solution)/shard_map/ppermute | solution.py:346
  18.9 1.1 %collective-permute-start.6 = (bf16[768,128]{1,0:T(8,128)(2,1)S(1)}, bf16[768,128]{1,0:T(8,128)(2,1)S(1)}, u32[]{:S(2)}, u32[]{:S(2)}) collective-permute-start(bf16[768,128]{1,0:T(8,128)(2,1)S(1)} %collective-permute-done.5.refs_11_), channel_id=1, source_target_pairs={{0,32},{32,0},{64,96},{96,64},{1,33},{33,1},{65,97},{97,65},{2,34}... | collective-permute-start | bytes 589832 | tf_op jit(solution)/shard_map/ppermute | solution.py:345
  20.4 2.6 %collective-permute-start.11 = (bf16[768,128]{1,0:T(8,128)(2,1)S(1)}, bf16[768,128]{1,0:T(8,128)(2,1)S(1)}, u32[]{:S(2)}, u32[]{:S(2)}) collective-permute-start(bf16[768,128]{1,0:T(8,128)(2,1)S(1)} %collective-permute-done.9.refs_13_), channel_id=1, source_target_pairs={{0,32},{32,0},{64,96},{96,64},{1,33},{33,1},{65,97},{97,65},{2,34}... | collective-permute-start | bytes 589832 | tf_op jit(solution)/shard_map/ppermute | solution.py:349
  23.0 2.0 %collective-permute-start.13 = (bf16[2,768,128]{2,1,0:T(8,128)(2,1)S(1)}, bf16[2,768,128]{2,1,0:T(8,128)(2,1)S(1)}, u32[]{:S(2)}, u32[]{:S(2)}) collective-permute-start(bf16[2,768,128]{2,1,0:T(8,128)(2,1)S(1)} %copy-done.7), channel_id=1, source_target_pairs={{0,8},{8,16},{16,24},{24,0},{1,9},{9,17},{17,25},{25,1},{2,10},{10... | collective-permute-start | bytes 1179656 | tf_op jit(solution)/shard_map/ppermute | solution.py:347
  25.0 2.8 %collective-permute-start.15 = (bf16[768,128]{1,0:T(8,128)(2,1)S(1)}, bf16[768,128]{1,0:T(8,128)(2,1)S(1)}, u32[]{:S(2)}, u32[]{:S(2)}) collective-permute-start(bf16[768,128]{1,0:T(8,128)(2,1)S(1)} %collective-permute-done.8.refs_11_), channel_id=1, source_target_pairs={{0,8},{8,16},{16,24},{24,0},{1,9},{9,17},{17,25},{25,1},{2,10},{10... | collective-permute-start | bytes 589832 | tf_op jit(solution)/shard_map/ppermute | solution.py:350
  27.9 12.7 %query_side.1 = (bf16[768,128]{1,0:T(8,128)(2,1)}, bf16[768,128]{1,0:T(8,128)(2,1)}, f32[8,256]{1,0:T(8,128)S(1)}) custom-call(s32[95]{0:T(128)S(1)} %copy-done.5, bf16[768,128]{1,0:T(8,128)(2,1)S(1)} %bitcast.24, bf16[768,128]{1,0:T(8,128)(2,1)S(1)} %bitcast.27, bf16[768,128]{1,0:T(8,128)(2,1)S(1)} %bitcast.21, bf16[768,128]{1,0:T(8,128)(2,1)S(1)} %bitcast.30, ...), custom_call_target="tpu_custom_call" | custom-call | flops 2684354560 | bytes 786432 | tf_op jit(solution)/shard_map/query_side/pallas_call | solution.py:270
  40.6 1.4 %collective-permute-start.22 = (f32[8,256]{1,0:T(8,128)S(1)}, f32[8,256]{1,0:T(8,128)S(1)}, u32[]{:S(2)}, u32[]{:S(2)}) collective-permute-start(f32[8,256]{1,0:T(8,128)S(1)} %get-tuple-element.41), channel_id=1, source_target_pairs={{0,32},{32,0},{64,96},{96,64},{1,33},{33,1},{65,97},{97,65},{2,34}... | collective-permute-start | bytes 24584 | tf_op jit(solution)/shard_map/ppermute | solution.py:249
  42.1 5.3 %collective-permute-start.23 = (f32[8,256]{1,0:T(8,128)S(1)}, f32[8,256]{1,0:T(8,128)S(1)}, u32[]{:S(2)}, u32[]{:S(2)}) collective-permute-start(f32[8,256]{1,0:T(8,128)S(1)} %get-tuple-element.41), channel_id=1, source_target_pairs={{0,0},{32,64},{64,32},{96,96},{1,1},{33,65},{65,33},{97,97},{2,2},... | collective-permute-start | bytes 24584 | tf_op jit(solution)/shard_map/ppermute | solution.py:249
  47.5 0.5 collective-permute-start.18
  48.0 0.7 %collective-permute-done.23 = f32[8,256]{1,0:T(8,128)S(1)} collective-permute-done((f32[8,256]{1,0:T(8,128)S(1)}, f32[8,256]{1,0:T(8,128)S(1)}, u32[]{:S(2)}, u32[]{:S(2)}) %collective-permute-start.23) | collective-permute-done | bytes 8224 | tf_op jit(solution)/shard_map/ppermute | solution.py:249
  48.8 2.7 %collective-permute-start.24 = (f32[24,256]{1,0:T(8,128)S(1)}, f32[24,256]{1,0:T(8,128)S(1)}, u32[]{:S(2)}, u32[]{:S(2)}) collective-permute-start(f32[24,256]{1,0:T(8,128)S(1)} %constant_dynamic-update-slice_fusion.refs_16_), channel_id=1, source_target_pairs={{0,8},{8,16},{16,24},{24,0},{1,9},{9,17},{17,25},{25,1},{2,10},{10... | collective-permute-start | bytes 73736 | tf_op jit(solution)/shard_map/ppermute | solution.py:250
  51.4 1.0 %collective-permute-done.24.refs_17_ = f32[24,256]{1,0:T(8,128)S(1)} collective-permute-done((f32[24,256]{1,0:T(8,128)S(1)}, f32[24,256]{1,0:T(8,128)S(1)}, u32[]{:S(2)}, u32[]{:S(2)}) %collective-permute-start.24) | collective-permute-done | bytes 24608 | tf_op jit(solution)/shard_map/ppermute | solution.py:250
  52.7 3.2 %collective-permute-done.25.refs_18_ = f32[24,256]{1,0:T(8,128)S(1)} collective-permute-done((f32[24,256]{1,0:T(8,128)S(1)}, f32[24,256]{1,0:T(8,128)S(1)}, u32[]{:S(2)}, u32[]{:S(2)}) %collective-permute-start.25) | collective-permute-done | bytes 24608 | tf_op jit(solution)/shard_map/ppermute | solution.py:250
  56.3 1.1 %collective-permute-done.21.refs_14_ = bf16[768,128]{1,0:T(8,128)(2,1)S(1)} collective-permute-done((bf16[768,128]{1,0:T(8,128)(2,1)S(1)}, bf16[768,128]{1,0:T(8,128)(2,1)S(1)}, u32[]{:S(2)}, u32[]{:S(2)}) %collective-permute-start.21) | collective-permute-done | bytes 196640 | tf_op jit(solution)/shard_map/ppermute | solution.py:358
  57.4 0.7 %copy-done.14 = bf16[2,768,128]{2,1,0:T(8,128)(2,1)} copy-done((bf16[2,768,128]{2,1,0:T(8,128)(2,1)}, bf16[2,768,128]{2,1,0:T(8,128)(2,1)S(1)}, u32[]{:S(2)}) %copy-start.14) | copy-done | bytes 393240
  58.2 11.9 %key_side.1 = (bf16[768,128]{1,0:T(8,128)(2,1)}, bf16[768,128]{1,0:T(8,128)(2,1)}) custom-call(s32[75]{0:T(128)S(1)} %copy-done.4, bf16[768,128]{1,0:T(8,128)(2,1)S(1)} %bitcast.22, bf16[768,128]{1,0:T(8,128)(2,1)S(1)} %bitcast.31, bf16[768,128]{1,0:T(8,128)(2,1)S(1)} %bitcast.25, bf16[768,128]{1,0:T(8,128)(2,1)S(1)} %bitcast.28, ...), custom_call_target="tpu_custom_call" | custom-call | flops 2147483648 | bytes 786432 | tf_op jit(solution)/shard_map/key_side/pallas_call | solution.py:295
  (72 shorter events, 2.3 us)
Async XLA Ops:
  3.6 6.4 %collective-permute-start.7 = (bf16[2,768,128]{2,1,0:T(8,128)(2,1)}, bf16[2,768,128]{2,1,0:T(8,128)(2,1)S(1)}, u32[]{:S(2)}, u32[]{:S(2)}) collective-permute-start(bf16[2,768,128]{2,1,0:T(8,128)(2,1)} %get-tuple-element.35), channel_id=1, source_target_pairs={{0,32},{32,0},{64,96},{96,64},{1,33},{33,1},{65,97},{97,65},{2,34}... | collective-permute-start | bytes 1179656 | tf_op jit(solution)/shard_map/ppermute | solution.py:341
  3.7 10.5 %collective-permute-start = (bf16[2,768,128]{2,1,0:T(8,128)(2,1)}, bf16[2,768,128]{2,1,0:T(8,128)(2,1)S(1)}, u32[]{:S(2)}, u32[]{:S(2)}) collective-permute-start(bf16[2,768,128]{2,1,0:T(8,128)(2,1)} %get-tuple-element.25), channel_id=1, source_target_pairs={{0,8},{8,16},{16,24},{24,0},{1,9},{9,17},{17,25},{25,1},{2,10},{10... | collective-permute-start | bytes 1179656 | tf_op jit(solution)/shard_map/ppermute | solution.py:337
  4.7 12.2 %collective-permute-start.1 = (bf16[2,768,128]{2,1,0:T(8,128)(2,1)}, bf16[2,768,128]{2,1,0:T(8,128)(2,1)S(1)}, u32[]{:S(2)}, u32[]{:S(2)}) collective-permute-start(bf16[2,768,128]{2,1,0:T(8,128)(2,1)} %get-tuple-element.25), channel_id=1, source_target_pairs={{0,24},{8,0},{16,8},{24,16},{1,25},{9,1},{17,9},{25,17},{2,26},{10... | collective-permute-start | bytes 1179656 | tf_op jit(solution)/shard_map/ppermute | solution.py:337
  6.3 9.1 %collective-permute-start.5 = (bf16[768,128]{1,0:T(8,128)(2,1)S(1)}, bf16[768,128]{1,0:T(8,128)(2,1)S(1)}, u32[]{:S(2)}, u32[]{:S(2)}) collective-permute-start(bf16[768,128]{1,0:T(8,128)(2,1)S(1)} %fusion.1), channel_id=1, source_target_pairs={{0,64},{32,96},{64,0},{96,32},{1,65},{33,97},{65,1},{97,33},{2,66}... | collective-permute-start | bytes 589832 | tf_op jit(solution)/shard_map/ppermute | solution.py:340
  10.0 8.9 %collective-permute-start.8 = (bf16[768,128]{1,0:T(8,128)(2,1)S(1)}, bf16[768,128]{1,0:T(8,128)(2,1)S(1)}, u32[]{:S(2)}, u32[]{:S(2)}) collective-permute-start(bf16[768,128]{1,0:T(8,128)(2,1)S(1)} %fusion), channel_id=1, source_target_pairs={{0,64},{32,96},{64,0},{96,32},{1,65},{33,97},{65,1},{97,33},{2,66}... | collective-permute-start | bytes 589832 | tf_op jit(solution)/shard_map/ppermute | solution.py:342
  14.1 10.8 %collective-permute-start.3 = (bf16[2,768,128]{2,1,0:T(8,128)(2,1)S(1)}, bf16[2,768,128]{2,1,0:T(8,128)(2,1)S(1)}, u32[]{:S(2)}, u32[]{:S(2)}) collective-permute-start(bf16[2,768,128]{2,1,0:T(8,128)(2,1)S(1)} %collective-permute-done.refs_5_), channel_id=1, source_target_pairs={{0,32},{32,0},{64,96},{96,64},{1,33},{33,1},{65,97},{97,65},{2,34}... | collective-permute-start | bytes 1179656 | tf_op jit(solution)/shard_map/ppermute | solution.py:346
  15.4 4.9 %collective-permute-start.10 = (bf16[768,128]{1,0:T(8,128)(2,1)S(1)}, bf16[768,128]{1,0:T(8,128)(2,1)S(1)}, u32[]{:S(2)}, u32[]{:S(2)}) collective-permute-start(bf16[768,128]{1,0:T(8,128)(2,1)S(1)} %collective-permute-done.5.refs_11_), channel_id=1, source_target_pairs={{0,24},{8,0},{16,8},{24,16},{1,25},{9,1},{17,9},{25,17},{2,26},{10... | collective-permute-start | bytes 589832 | tf_op jit(solution)/shard_map/ppermute | solution.py:344
  15.6 4.8 %collective-permute-start.9 = (bf16[768,128]{1,0:T(8,128)(2,1)S(1)}, bf16[768,128]{1,0:T(8,128)(2,1)S(1)}, u32[]{:S(2)}, u32[]{:S(2)}) collective-permute-start(bf16[768,128]{1,0:T(8,128)(2,1)S(1)} %collective-permute-done.5.refs_11_), channel_id=1, source_target_pairs={{0,8},{8,16},{16,24},{24,0},{1,9},{9,17},{17,25},{25,1},{2,10},{10... | collective-permute-start | bytes 589832 | tf_op jit(solution)/shard_map/ppermute | solution.py:344
  16.9 8.1 %collective-permute-start.4 = (bf16[2,768,128]{2,1,0:T(8,128)(2,1)S(1)}, bf16[2,768,128]{2,1,0:T(8,128)(2,1)S(1)}, u32[]{:S(2)}, u32[]{:S(2)}) collective-permute-start(bf16[2,768,128]{2,1,0:T(8,128)(2,1)S(1)} %collective-permute-done.1.refs_6_), channel_id=1, source_target_pairs={{0,32},{32,0},{64,96},{96,64},{1,33},{33,1},{65,97},{97,65},{2,34}... | collective-permute-start | bytes 1179656 | tf_op jit(solution)/shard_map/ppermute | solution.py:346
  18.9 4.1 %collective-permute-start.6 = (bf16[768,128]{1,0:T(8,128)(2,1)S(1)}, bf16[768,128]{1,0:T(8,128)(2,1)S(1)}, u32[]{:S(2)}, u32[]{:S(2)}) collective-permute-start(bf16[768,128]{1,0:T(8,128)(2,1)S(1)} %collective-permute-done.5.refs_11_), channel_id=1, source_target_pairs={{0,32},{32,0},{64,96},{96,64},{1,33},{33,1},{65,97},{97,65},{2,34}... | collective-permute-start | bytes 589832 | tf_op jit(solution)/shard_map/ppermute | solution.py:345
  20.4 7.4 %collective-permute-start.11 = (bf16[768,128]{1,0:T(8,128)(2,1)S(1)}, bf16[768,128]{1,0:T(8,128)(2,1)S(1)}, u32[]{:S(2)}, u32[]{:S(2)}) collective-permute-start(bf16[768,128]{1,0:T(8,128)(2,1)S(1)} %collective-permute-done.9.refs_13_), channel_id=1, source_target_pairs={{0,32},{32,0},{64,96},{96,64},{1,33},{33,1},{65,97},{97,65},{2,34}... | collective-permute-start | bytes 589832 | tf_op jit(solution)/shard_map/ppermute | solution.py:349
  23.0 4.8 %collective-permute-start.12 = (bf16[768,128]{1,0:T(8,128)(2,1)S(1)}, bf16[768,128]{1,0:T(8,128)(2,1)S(1)}, u32[]{:S(2)}, u32[]{:S(2)}) collective-permute-start(bf16[768,128]{1,0:T(8,128)(2,1)S(1)} %collective-permute-done.10.refs_15_), channel_id=1, source_target_pairs={{0,32},{32,0},{64,96},{96,64},{1,33},{33,1},{65,97},{97,65},{2,34}... | collective-permute-start | bytes 589832 | tf_op jit(solution)/shard_map/ppermute | solution.py:349
  23.0 17.7 %collective-permute-start.13 = (bf16[2,768,128]{2,1,0:T(8,128)(2,1)S(1)}, bf16[2,768,128]{2,1,0:T(8,128)(2,1)S(1)}, u32[]{:S(2)}, u32[]{:S(2)}) collective-permute-start(bf16[2,768,128]{2,1,0:T(8,128)(2,1)S(1)} %copy-done.7), channel_id=1, source_target_pairs={{0,8},{8,16},{16,24},{24,0},{1,9},{9,17},{17,25},{25,1},{2,10},{10... | collective-permute-start | bytes 1179656 | tf_op jit(solution)/shard_map/ppermute | solution.py:347
  24.9 15.7 %collective-permute-start.14 = (bf16[2,768,128]{2,1,0:T(8,128)(2,1)S(1)}, bf16[2,768,128]{2,1,0:T(8,128)(2,1)S(1)}, u32[]{:S(2)}, u32[]{:S(2)}) collective-permute-start(bf16[2,768,128]{2,1,0:T(8,128)(2,1)S(1)} %copy-done.7), channel_id=1, source_target_pairs={{0,24},{8,0},{16,8},{24,16},{1,25},{9,1},{17,9},{25,17},{2,26},{10... | collective-permute-start | bytes 1179656 | tf_op jit(solution)/shard_map/ppermute | solution.py:347
  25.0 15.6 %collective-permute-start.15 = (bf16[768,128]{1,0:T(8,128)(2,1)S(1)}, bf16[768,128]{1,0:T(8,128)(2,1)S(1)}, u32[]{:S(2)}, u32[]{:S(2)}) collective-permute-start(bf16[768,128]{1,0:T(8,128)(2,1)S(1)} %collective-permute-done.8.refs_11_), channel_id=1, source_target_pairs={{0,8},{8,16},{16,24},{24,0},{1,9},{9,17},{17,25},{25,1},{2,10},{10... | collective-permute-start | bytes 589832 | tf_op jit(solution)/shard_map/ppermute | solution.py:350
  27.8 12.8 %collective-permute-start.16 = (bf16[768,128]{1,0:T(8,128)(2,1)S(1)}, bf16[768,128]{1,0:T(8,128)(2,1)S(1)}, u32[]{:S(2)}, u32[]{:S(2)}) collective-permute-start(bf16[768,128]{1,0:T(8,128)(2,1)S(1)} %collective-permute-done.8.refs_11_), channel_id=1, source_target_pairs={{0,24},{8,0},{16,8},{24,16},{1,25},{9,1},{17,9},{25,17},{2,26},{10... | collective-permute-start | bytes 589832 | tf_op jit(solution)/shard_map/ppermute | solution.py:350
  40.6 7.4 %collective-permute-start.22 = (f32[8,256]{1,0:T(8,128)S(1)}, f32[8,256]{1,0:T(8,128)S(1)}, u32[]{:S(2)}, u32[]{:S(2)}) collective-permute-start(f32[8,256]{1,0:T(8,128)S(1)} %get-tuple-element.41), channel_id=1, source_target_pairs={{0,32},{32,0},{64,96},{96,64},{1,33},{33,1},{65,97},{97,65},{2,34}... | collective-permute-start | bytes 24584 | tf_op jit(solution)/shard_map/ppermute | solution.py:249
  42.1 6.7 %collective-permute-start.23 = (f32[8,256]{1,0:T(8,128)S(1)}, f32[8,256]{1,0:T(8,128)S(1)}, u32[]{:S(2)}, u32[]{:S(2)}) collective-permute-start(f32[8,256]{1,0:T(8,128)S(1)} %get-tuple-element.41), channel_id=1, source_target_pairs={{0,0},{32,64},{64,32},{96,96},{1,1},{33,65},{65,33},{97,97},{2,2},... | collective-permute-start | bytes 24584 | tf_op jit(solution)/shard_map/ppermute | solution.py:249
  47.4 9.9 %collective-permute-start.17 = (bf16[2,768,128]{2,1,0:T(8,128)(2,1)S(1)}, bf16[2,768,128]{2,1,0:T(8,128)(2,1)S(1)}, u32[]{:S(2)}, u32[]{:S(2)}) collective-permute-start(bf16[2,768,128]{2,1,0:T(8,128)(2,1)S(1)} %collective-permute-done.13.refs_5_), channel_id=1, source_target_pairs={{0,32},{32,0},{64,96},{96,64},{1,33},{33,1},{65,97},{97,65},{2,34}... | collective-permute-start | bytes 1179656 | tf_op jit(solution)/shard_map/ppermute | solution.py:357
  47.5 9.8 %collective-permute-start.18 = (bf16[2,768,128]{2,1,0:T(8,128)(2,1)S(1)}, bf16[2,768,128]{2,1,0:T(8,128)(2,1)S(1)}, u32[]{:S(2)}, u32[]{:S(2)}) collective-permute-start(bf16[2,768,128]{2,1,0:T(8,128)(2,1)S(1)} %collective-permute-done.14.refs_6_), channel_id=1, source_target_pairs={{0,32},{32,0},{64,96},{96,64},{1,33},{33,1},{65,97},{97,65},{2,34}... | collective-permute-start | bytes 1179656 | tf_op jit(solution)/shard_map/ppermute | solution.py:357
  48.8 3.7 %collective-permute-start.24 = (f32[24,256]{1,0:T(8,128)S(1)}, f32[24,256]{1,0:T(8,128)S(1)}, u32[]{:S(2)}, u32[]{:S(2)}) collective-permute-start(f32[24,256]{1,0:T(8,128)S(1)} %constant_dynamic-update-slice_fusion.refs_16_), channel_id=1, source_target_pairs={{0,8},{8,16},{16,24},{24,0},{1,9},{9,17},{17,25},{25,1},{2,10},{10... | collective-permute-start | bytes 73736 | tf_op jit(solution)/shard_map/ppermute | solution.py:250
  51.4 4.4 %collective-permute-start.25 = (f32[24,256]{1,0:T(8,128)S(1)}, f32[24,256]{1,0:T(8,128)S(1)}, u32[]{:S(2)}, u32[]{:S(2)}) collective-permute-start(f32[24,256]{1,0:T(8,128)S(1)} %constant_dynamic-update-slice_fusion.refs_16_), channel_id=1, source_target_pairs={{0,24},{8,0},{16,8},{24,16},{1,25},{9,1},{17,9},{25,17},{2,26},{10... | collective-permute-start | bytes 73736 | tf_op jit(solution)/shard_map/ppermute | solution.py:250
  51.4 4.8 %collective-permute-start.19 = (bf16[768,128]{1,0:T(8,128)(2,1)S(1)}, bf16[768,128]{1,0:T(8,128)(2,1)S(1)}, u32[]{:S(2)}, u32[]{:S(2)}) collective-permute-start(bf16[768,128]{1,0:T(8,128)(2,1)S(1)} %collective-permute-done.8.refs_11_), channel_id=1, source_target_pairs={{0,32},{32,0},{64,96},{96,64},{1,33},{33,1},{65,97},{97,65},{2,34}... | collective-permute-start | bytes 589832 | tf_op jit(solution)/shard_map/ppermute | solution.py:358
  52.5 3.8 %collective-permute-start.20 = (bf16[768,128]{1,0:T(8,128)(2,1)S(1)}, bf16[768,128]{1,0:T(8,128)(2,1)S(1)}, u32[]{:S(2)}, u32[]{:S(2)}) collective-permute-start(bf16[768,128]{1,0:T(8,128)(2,1)S(1)} %collective-permute-done.15.refs_13_), channel_id=1, source_target_pairs={{0,32},{32,0},{64,96},{96,64},{1,33},{33,1},{65,97},{97,65},{2,34}... | collective-permute-start | bytes 589832 | tf_op jit(solution)/shard_map/ppermute | solution.py:358
  (20 other events, 243.6 us)

commit v3 on v2

--- a/solution.py
+++ b/solution.py
@@ -305,7 +305,7 @@
             pltpu.SemaphoreType.DMA((SLOTS + 6,)),
             *[pltpu.VMEM((tile, SUB * tile), BF16)] * (2 * TURN),
         ],
-        compiler_params=PARAMS,
+        compiler_params=pltpu.CompilerParams(vmem_limit_bytes=24 * 2**20),
         cost_estimate=pl.CostEstimate(
             flops=32 * 4 * 2 * tile * tile * width, bytes_accessed=8 * tokens * width, transcendentals=32 * tile * tile
         ),

time: 70.6 us -> 70.5 us (level)
  the two profiles are of different devices: /device:TPU:17 before, /device:TPU:70 now
where the time goes in v3:
time: 70.5 us; the launch traced here: 69.6 us
  Pallas kernels  25.2 us (36%)
  starting transfers between devices  22.8 us (32%)
  waiting for transfers between devices  19.4 us (28%)
  other arithmetic  1.13 us (2%)
  between operations  0.91 us (1%)
    pallas_call x1, Pallas kernels, query_call(): pl.pallas_call(lambda *refs: query_kernel(columns, tile, scale, *refs), o...  12.7 us
    pallas_call x1, Pallas kernels, key_call(): pl.pallas_call(lambda *refs: key_kernel(columns, tile, scale, *refs), out...  10.4 us
    ppermute x2, waiting for transfers between devices, body(): half_up, half_down = (send(half, ROWS, before), send(half, ROWS, after))  6 us
    ppermute x2, waiting for transfers between devices, body(): kv_up, kv_down = (send(kv, ROWS, before), send(kv, ROWS, after))  4.46 us
    ppermute x1, waiting for transfers between devices, spread_small(): lax.ppermute(x, TM, far)  3.95 us
    ppermute x1, starting transfers between devices, body(): qg_half = send(jnp.where(inner, qg[0], qg_o[1]), TM, ring(TM, 2))  3.58 us
    ppermute x2, starting transfers between devices, body(): kv_up, kv_down = (send(kv, ROWS, before), send(kv, ROWS, after))  3.24 us
    ppermute x1, starting transfers between devices, spread_small(): lax.ppermute(frames, ROWS, after)  3.23 us
  transfers between devices with their start and end apart: 26, of which 9 were waited for; matrix products, arithmetic and copies ran while one was open for 2% of the time, Pallas kernels for 18%

profile of v3, /device:TPU:70, one launch (start us, length us, event | category | flops | bytes accessed | tf_op | source)
XLA Modules:
  0.0 69.6 jit_solution(9352809175117543811)
XLA Ops:
  0.6 2.2 %pack.1 = (bf16[2,768,128]{2,1,0:T(8,128)(2,1)}, bf16[2,768,128]{2,1,0:T(8,128)(2,1)}, s32[95]{0:T(128)}, s32[75]{0:T(128)}) custom-call(s32[1,1,3,1,27]{4,3,2,1,0:T(1,128)} %refs_0_.1, bf16[768,128]{1,0:T(8,128)(2,1)} %bitcast.20, bf16[768,128]{1,0:T(8,128)(2,1)} %bitcast.23, bf16[768,128]{1,0:T(8,128)(2,1)} %bitcast.26, bf16[768,128]{1,0:T(8,128)(2,1)} %bitcast.29), custom_call_target="tpu_custom_call" | custom-call | tf_op jit(solution)/shard_map/pack/pallas_call | solution.py:323
  2.9 0.5 collective-permute-start.7
  3.4 1.6 %collective-permute-start = (bf16[2,768,128]{2,1,0:T(8,128)(2,1)}, bf16[2,768,128]{2,1,0:T(8,128)(2,1)S(1)}, u32[]{:S(2)}, u32[]{:S(2)}) collective-permute-start(bf16[2,768,128]{2,1,0:T(8,128)(2,1)} %get-tuple-element.25), channel_id=1, source_target_pairs={{0,8},{8,16},{16,24},{24,0},{1,9},{9,17},{17,25},{25,1},{2,10},{10... | collective-permute-start | bytes 1179656 | tf_op jit(solution)/shard_map/ppermute | solution.py:337
  5.0 1.7 %collective-permute-start.1 = (bf16[2,768,128]{2,1,0:T(8,128)(2,1)}, bf16[2,768,128]{2,1,0:T(8,128)(2,1)S(1)}, u32[]{:S(2)}, u32[]{:S(2)}) collective-permute-start(bf16[2,768,128]{2,1,0:T(8,128)(2,1)} %get-tuple-element.25), channel_id=1, source_target_pairs={{0,24},{8,0},{16,8},{24,16},{1,25},{9,1},{17,9},{25,17},{2,26},{10... | collective-permute-start | bytes 1179656 | tf_op jit(solution)/shard_map/ppermute | solution.py:337
  6.7 1.1 %fusion.1 = bf16[768,128]{1,0:T(8,128)(2,1)S(1)} fusion(bf16[2,768,128]{2,1,0:T(8,128)(2,1)S(1)} %collective-permute-done.2.refs_7_, bf16[2,768,128]{2,1,0:T(8,128)(2,1)} %get-tuple-element.25, pred[]{:T(512)S(6)} %and.4), kind=kLoop, calls=%fused_computation.3 | loop fusion | flops 98304 | bytes 589825 | tf_op jit(solution)/shard_map/jit(_where)/select_n | solution.py:340
  8.0 3.6 %collective-permute-start.8 = (bf16[768,128]{1,0:T(8,128)(2,1)S(1)}, bf16[768,128]{1,0:T(8,128)(2,1)S(1)}, u32[]{:S(2)}, u32[]{:S(2)}) collective-permute-start(bf16[768,128]{1,0:T(8,128)(2,1)S(1)} %fusion), channel_id=1, source_target_pairs={{0,64},{32,96},{64,0},{96,32},{1,65},{33,97},{65,1},{97,33},{2,66}... | collective-permute-start | bytes 589832 | tf_op jit(solution)/shard_map/ppermute | solution.py:342
  11.5 4.5 %collective-permute-done.refs_5_ = bf16[2,768,128]{2,1,0:T(8,128)(2,1)S(1)} collective-permute-done((bf16[2,768,128]{2,1,0:T(8,128)(2,1)}, bf16[2,768,128]{2,1,0:T(8,128)(2,1)S(1)}, u32[]{:S(2)}, u32[]{:S(2)}) %collective-permute-start) | collective-permute-done | bytes 393248 | tf_op jit(solution)/shard_map/ppermute | solution.py:337
  16.0 1.2 %collective-permute-done.5.refs_11_ = bf16[768,128]{1,0:T(8,128)(2,1)S(1)} collective-permute-done((bf16[768,128]{1,0:T(8,128)(2,1)S(1)}, bf16[768,128]{1,0:T(8,128)(2,1)S(1)}, u32[]{:S(2)}, u32[]{:S(2)}) %collective-permute-start.5) | collective-permute-done | bytes 196640 | tf_op jit(solution)/shard_map/ppermute | solution.py:340
  17.2 1.8 %collective-permute-start.10 = (bf16[768,128]{1,0:T(8,128)(2,1)S(1)}, bf16[768,128]{1,0:T(8,128)(2,1)S(1)}, u32[]{:S(2)}, u32[]{:S(2)}) collective-permute-start(bf16[768,128]{1,0:T(8,128)(2,1)S(1)} %collective-permute-done.5.refs_11_), channel_id=1, source_target_pairs={{0,24},{8,0},{16,8},{24,16},{1,25},{9,1},{17,9},{25,17},{2,26},{10... | collective-permute-start | bytes 589832 | tf_op jit(solution)/shard_map/ppermute | solution.py:344
  19.2 0.8 %collective-permute-done.8.refs_11_ = bf16[768,128]{1,0:T(8,128)(2,1)S(1)} collective-permute-done((bf16[768,128]{1,0:T(8,128)(2,1)S(1)}, bf16[768,128]{1,0:T(8,128)(2,1)S(1)}, u32[]{:S(2)}, u32[]{:S(2)}) %collective-permute-start.8) | collective-permute-done | bytes 196640 | tf_op jit(solution)/shard_map/ppermute | solution.py:342
  20.0 3.3 %collective-permute-done.10.refs_15_ = bf16[768,128]{1,0:T(8,128)(2,1)S(1)} collective-permute-done((bf16[768,128]{1,0:T(8,128)(2,1)S(1)}, bf16[768,128]{1,0:T(8,128)(2,1)S(1)}, u32[]{:S(2)}, u32[]{:S(2)}) %collective-permute-start.10) | collective-permute-done | bytes 196640 | tf_op jit(solution)/shard_map/ppermute | solution.py:344
  23.3 2.7 %collective-permute-done.9.refs_13_ = bf16[768,128]{1,0:T(8,128)(2,1)S(1)} collective-permute-done((bf16[768,128]{1,0:T(8,128)(2,1)S(1)}, bf16[768,128]{1,0:T(8,128)(2,1)S(1)}, u32[]{:S(2)}, u32[]{:S(2)}) %collective-permute-start.9) | collective-permute-done | bytes 196640 | tf_op jit(solution)/shard_map/ppermute | solution.py:344
  26.0 0.5 collective-permute-start.12
  26.5 3.2 %collective-permute-start.14 = (bf16[2,768,128]{2,1,0:T(8,128)(2,1)S(1)}, bf16[2,768,128]{2,1,0:T(8,128)(2,1)S(1)}, u32[]{:S(2)}, u32[]{:S(2)}) collective-permute-start(bf16[2,768,128]{2,1,0:T(8,128)(2,1)S(1)} %copy-done.6), channel_id=1, source_target_pairs={{0,24},{8,0},{16,8},{24,16},{1,25},{9,1},{17,9},{25,17},{2,26},{10... | collective-permute-start | bytes 1179656 | tf_op jit(solution)/shard_map/ppermute | solution.py:347
  29.8 3.2 %collective-permute-start.16 = (bf16[768,128]{1,0:T(8,128)(2,1)S(1)}, bf16[768,128]{1,0:T(8,128)(2,1)S(1)}, u32[]{:S(2)}, u32[]{:S(2)}) collective-permute-start(bf16[768,128]{1,0:T(8,128)(2,1)S(1)} %collective-permute-done.8.refs_11_), channel_id=1, source_target_pairs={{0,24},{8,0},{16,8},{24,16},{1,25},{9,1},{17,9},{25,17},{2,26},{10... | collective-permute-start | bytes 589832 | tf_op jit(solution)/shard_map/ppermute | solution.py:350
  33.1 12.7 %query_side.1 = (bf16[768,128]{1,0:T(8,128)(2,1)}, bf16[768,128]{1,0:T(8,128)(2,1)}, f32[8,256]{1,0:T(8,128)S(1)}) custom-call(s32[95]{0:T(128)S(1)} %copy-done.5, bf16[768,128]{1,0:T(8,128)(2,1)S(1)} %bitcast.24, bf16[768,128]{1,0:T(8,128)(2,1)S(1)} %bitcast.27, bf16[768,128]{1,0:T(8,128)(2,1)S(1)} %bitcast.21, bf16[768,128]{1,0:T(8,128)(2,1)S(1)} %bitcast.30, ...), custom_call_target="tpu_custom_call" | custom-call | flops 2684354560 | bytes 786432 | tf_op jit(solution)/shard_map/query_side/pallas_call | solution.py:270
  45.9 1.9 %collective-permute-start.23 = (f32[8,256]{1,0:T(8,128)S(1)}, f32[8,256]{1,0:T(8,128)S(1)}, u32[]{:S(2)}, u32[]{:S(2)}) collective-permute-start(f32[8,256]{1,0:T(8,128)S(1)} %get-tuple-element.41), channel_id=1, source_target_pairs={{0,0},{32,64},{64,32},{96,96},{1,1},{33,65},{65,33},{97,97},{2,2},... | collective-permute-start | bytes 24584 | tf_op jit(solution)/shard_map/ppermute | solution.py:249
  47.9 0.5 collective-permute-start.18
  48.4 3.9 %collective-permute-done.23 = f32[8,256]{1,0:T(8,128)S(1)} collective-permute-done((f32[8,256]{1,0:T(8,128)S(1)}, f32[8,256]{1,0:T(8,128)S(1)}, u32[]{:S(2)}, u32[]{:S(2)}) %collective-permute-start.23) | collective-permute-done | bytes 8224 | tf_op jit(solution)/shard_map/ppermute | solution.py:249
  52.4 3.2 %collective-permute-start.25 = (f32[24,256]{1,0:T(8,128)S(1)}, f32[24,256]{1,0:T(8,128)S(1)}, u32[]{:S(2)}, u32[]{:S(2)}) collective-permute-start(f32[24,256]{1,0:T(8,128)S(1)} %constant_dynamic-update-slice_fusion.refs_16_), channel_id=1, source_target_pairs={{0,24},{8,0},{16,8},{24,16},{1,25},{9,1},{17,9},{25,17},{2,26},{10... | collective-permute-start | bytes 73736 | tf_op jit(solution)/shard_map/ppermute | solution.py:250
  55.6 1.8 %collective-permute-done.24.refs_17_ = f32[24,256]{1,0:T(8,128)S(1)} collective-permute-done((f32[24,256]{1,0:T(8,128)S(1)}, f32[24,256]{1,0:T(8,128)S(1)}, u32[]{:S(2)}, u32[]{:S(2)}) %collective-permute-start.24) | collective-permute-done | bytes 24608 | tf_op jit(solution)/shard_map/ppermute | solution.py:250
  57.4 0.5 collective-permute-start.21
  57.9 0.9 %collective-permute-done.20.refs_12_ = bf16[768,128]{1,0:T(8,128)(2,1)S(1)} collective-permute-done((bf16[768,128]{1,0:T(8,128)(2,1)S(1)}, bf16[768,128]{1,0:T(8,128)(2,1)S(1)}, u32[]{:S(2)}, u32[]{:S(2)}) %collective-permute-start.20) | collective-permute-done | bytes 196640 | tf_op jit(solution)/shard_map/ppermute | solution.py:358
  59.1 10.4 %key_side.1 = (bf16[768,128]{1,0:T(8,128)(2,1)}, bf16[768,128]{1,0:T(8,128)(2,1)}) custom-call(s32[75]{0:T(128)S(1)} %copy-done.4, bf16[768,128]{1,0:T(8,128)(2,1)S(1)} %bitcast.22, bf16[768,128]{1,0:T(8,128)(2,1)S(1)} %bitcast.31, bf16[768,128]{1,0:T(8,128)(2,1)S(1)} %bitcast.25, bf16[768,128]{1,0:T(8,128)(2,1)S(1)} %bitcast.28, ...), custom_call_target="tpu_custom_call" | custom-call | flops 2147483648 | bytes 786432 | tf_op jit(solution)/shard_map/key_side/pallas_call | solution.py:295
  (60 shorter events, 1.0 us)
Async XLA Ops:
  2.8 3.8 %collective-permute-start.2 = (bf16[2,768,128]{2,1,0:T(8,128)(2,1)}, bf16[2,768,128]{2,1,0:T(8,128)(2,1)S(1)}, u32[]{:S(2)}, u32[]{:S(2)}) collective-permute-start(bf16[2,768,128]{2,1,0:T(8,128)(2,1)} %get-tuple-element.25), channel_id=1, source_target_pairs={{0,32},{32,0},{64,96},{96,64},{1,33},{33,1},{65,97},{97,65},{2,34}... | collective-permute-start | bytes 1179656 | tf_op jit(solution)/shard_map/ppermute | solution.py:336
  2.9 5.0 %collective-permute-start.7 = (bf16[2,768,128]{2,1,0:T(8,128)(2,1)}, bf16[2,768,128]{2,1,0:T(8,128)(2,1)S(1)}, u32[]{:S(2)}, u32[]{:S(2)}) collective-permute-start(bf16[2,768,128]{2,1,0:T(8,128)(2,1)} %get-tuple-element.35), channel_id=1, source_target_pairs={{0,32},{32,0},{64,96},{96,64},{1,33},{33,1},{65,97},{97,65},{2,34}... | collective-permute-start | bytes 1179656 | tf_op jit(solution)/shard_map/ppermute | solution.py:341
  3.4 12.6 %collective-permute-start = (bf16[2,768,128]{2,1,0:T(8,128)(2,1)}, bf16[2,768,128]{2,1,0:T(8,128)(2,1)S(1)}, u32[]{:S(2)}, u32[]{:S(2)}) collective-permute-start(bf16[2,768,128]{2,1,0:T(8,128)(2,1)} %get-tuple-element.25), channel_id=1, source_target_pairs={{0,8},{8,16},{16,24},{24,0},{1,9},{9,17},{17,25},{25,1},{2,10},{10... | collective-permute-start | bytes 1179656 | tf_op jit(solution)/shard_map/ppermute | solution.py:337
  5.0 14.2 %collective-permute-start.1 = (bf16[2,768,128]{2,1,0:T(8,128)(2,1)}, bf16[2,768,128]{2,1,0:T(8,128)(2,1)S(1)}, u32[]{:S(2)}, u32[]{:S(2)}) collective-permute-start(bf16[2,768,128]{2,1,0:T(8,128)(2,1)} %get-tuple-element.25), channel_id=1, source_target_pairs={{0,24},{8,0},{16,8},{24,16},{1,25},{9,1},{17,9},{25,17},{2,26},{10... | collective-permute-start | bytes 1179656 | tf_op jit(solution)/shard_map/ppermute | solution.py:337
  7.8 9.4 %collective-permute-start.5 = (bf16[768,128]{1,0:T(8,128)(2,1)S(1)}, bf16[768,128]{1,0:T(8,128)(2,1)S(1)}, u32[]{:S(2)}, u32[]{:S(2)}) collective-permute-start(bf16[768,128]{1,0:T(8,128)(2,1)S(1)} %fusion.1), channel_id=1, source_target_pairs={{0,64},{32,96},{64,0},{96,32},{1,65},{33,97},{65,1},{97,33},{2,66}... | collective-permute-start | bytes 589832 | tf_op jit(solution)/shard_map/ppermute | solution.py:340
  8.0 12.0 %collective-permute-start.8 = (bf16[768,128]{1,0:T(8,128)(2,1)S(1)}, bf16[768,128]{1,0:T(8,128)(2,1)S(1)}, u32[]{:S(2)}, u32[]{:S(2)}) collective-permute-start(bf16[768,128]{1,0:T(8,128)(2,1)S(1)} %fusion), channel_id=1, source_target_pairs={{0,64},{32,96},{64,0},{96,32},{1,65},{33,97},{65,1},{97,33},{2,66}... | collective-permute-start | bytes 589832 | tf_op jit(solution)/shard_map/ppermute | solution.py:342
  16.0 10.5 %collective-permute-start.3 = (bf16[2,768,128]{2,1,0:T(8,128)(2,1)S(1)}, bf16[2,768,128]{2,1,0:T(8,128)(2,1)S(1)}, u32[]{:S(2)}, u32[]{:S(2)}) collective-permute-start(bf16[2,768,128]{2,1,0:T(8,128)(2,1)S(1)} %collective-permute-done.refs_5_), channel_id=1, source_target_pairs={{0,32},{32,0},{64,96},{96,64},{1,33},{33,1},{65,97},{97,65},{2,34}... | collective-permute-start | bytes 1179656 | tf_op jit(solution)/shard_map/ppermute | solution.py:346
  17.2 6.1 %collective-permute-start.10 = (bf16[768,128]{1,0:T(8,128)(2,1)S(1)}, bf16[768,128]{1,0:T(8,128)(2,1)S(1)}, u32[]{:S(2)}, u32[]{:S(2)}) collective-permute-start(bf16[768,128]{1,0:T(8,128)(2,1)S(1)} %collective-permute-done.5.refs_11_), channel_id=1, source_target_pairs={{0,24},{8,0},{16,8},{24,16},{1,25},{9,1},{17,9},{25,17},{2,26},{10... | collective-permute-start | bytes 589832 | tf_op jit(solution)/shard_map/ppermute | solution.py:344
  19.0 7.0 %collective-permute-start.9 = (bf16[768,128]{1,0:T(8,128)(2,1)S(1)}, bf16[768,128]{1,0:T(8,128)(2,1)S(1)}, u32[]{:S(2)}, u32[]{:S(2)}) collective-permute-start(bf16[768,128]{1,0:T(8,128)(2,1)S(1)} %collective-permute-done.5.refs_11_), channel_id=1, source_target_pairs={{0,8},{8,16},{16,24},{24,0},{1,9},{9,17},{17,25},{25,1},{2,10},{10... | collective-permute-start | bytes 589832 | tf_op jit(solution)/shard_map/ppermute | solution.py:344
  19.2 10.5 %collective-permute-start.4 = (bf16[2,768,128]{2,1,0:T(8,128)(2,1)S(1)}, bf16[2,768,128]{2,1,0:T(8,128)(2,1)S(1)}, u32[]{:S(2)}, u32[]{:S(2)}) collective-permute-start(bf16[2,768,128]{2,1,0:T(8,128)(2,1)S(1)} %collective-permute-done.1.refs_6_), channel_id=1, source_target_pairs={{0,32},{32,0},{64,96},{96,64},{1,33},{33,1},{65,97},{97,65},{2,34}... | collective-permute-start | bytes 1179656 | tf_op jit(solution)/shard_map/ppermute | solution.py:346
  20.0 6.5 %collective-permute-start.6 = (bf16[768,128]{1,0:T(8,128)(2,1)S(1)}, bf16[768,128]{1,0:T(8,128)(2,1)S(1)}, u32[]{:S(2)}, u32[]{:S(2)}) collective-permute-start(bf16[768,128]{1,0:T(8,128)(2,1)S(1)} %collective-permute-done.5.refs_11_), channel_id=1, source_target_pairs={{0,32},{32,0},{64,96},{96,64},{1,33},{33,1},{65,97},{97,65},{2,34}... | collective-permute-start | bytes 589832 | tf_op jit(solution)/shard_map/ppermute | solution.py:345
  26.0 3.8 %collective-permute-start.11 = (bf16[768,128]{1,0:T(8,128)(2,1)S(1)}, bf16[768,128]{1,0:T(8,128)(2,1)S(1)}, u32[]{:S(2)}, u32[]{:S(2)}) collective-permute-start(bf16[768,128]{1,0:T(8,128)(2,1)S(1)} %collective-permute-done.9.refs_13_), channel_id=1, source_target_pairs={{0,32},{32,0},{64,96},{96,64},{1,33},{33,1},{65,97},{97,65},{2,34}... | collective-permute-start | bytes 589832 | tf_op jit(solution)/shard_map/ppermute | solution.py:349
  26.0 7.0 %collective-permute-start.12 = (bf16[768,128]{1,0:T(8,128)(2,1)S(1)}, bf16[768,128]{1,0:T(8,128)(2,1)S(1)}, u32[]{:S(2)}, u32[]{:S(2)}) collective-permute-start(bf16[768,128]{1,0:T(8,128)(2,1)S(1)} %collective-permute-done.10.refs_15_), channel_id=1, source_target_pairs={{0,32},{32,0},{64,96},{96,64},{1,33},{33,1},{65,97},{97,65},{2,34}... | collective-permute-start | bytes 589832 | tf_op jit(solution)/shard_map/ppermute | solution.py:349
  26.5 19.3 %collective-permute-start.13 = (bf16[2,768,128]{2,1,0:T(8,128)(2,1)S(1)}, bf16[2,768,128]{2,1,0:T(8,128)(2,1)S(1)}, u32[]{:S(2)}, u32[]{:S(2)}) collective-permute-start(bf16[2,768,128]{2,1,0:T(8,128)(2,1)S(1)} %copy-done.6), channel_id=1, source_target_pairs={{0,8},{8,16},{16,24},{24,0},{1,9},{9,17},{17,25},{25,1},{2,10},{10... | collective-permute-start | bytes 1179656 | tf_op jit(solution)/shard_map/ppermute | solution.py:347
  26.5 19.2 %collective-permute-start.14 = (bf16[2,768,128]{2,1,0:T(8,128)(2,1)S(1)}, bf16[2,768,128]{2,1,0:T(8,128)(2,1)S(1)}, u32[]{:S(2)}, u32[]{:S(2)}) collective-permute-start(bf16[2,768,128]{2,1,0:T(8,128)(2,1)S(1)} %copy-done.6), channel_id=1, source_target_pairs={{0,24},{8,0},{16,8},{24,16},{1,25},{9,1},{17,9},{25,17},{2,26},{10... | collective-permute-start | bytes 1179656 | tf_op jit(solution)/shard_map/ppermute | solution.py:347
  29.8 16.0 %collective-permute-start.15 = (bf16[768,128]{1,0:T(8,128)(2,1)S(1)}, bf16[768,128]{1,0:T(8,128)(2,1)S(1)}, u32[]{:S(2)}, u32[]{:S(2)}) collective-permute-start(bf16[768,128]{1,0:T(8,128)(2,1)S(1)} %collective-permute-done.8.refs_11_), channel_id=1, source_target_pairs={{0,8},{8,16},{16,24},{24,0},{1,9},{9,17},{17,25},{25,1},{2,10},{10... | collective-permute-start | bytes 589832 | tf_op jit(solution)/shard_map/ppermute | solution.py:350
  29.8 16.0 %collective-permute-start.16 = (bf16[768,128]{1,0:T(8,128)(2,1)S(1)}, bf16[768,128]{1,0:T(8,128)(2,1)S(1)}, u32[]{:S(2)}, u32[]{:S(2)}) collective-permute-start(bf16[768,128]{1,0:T(8,128)(2,1)S(1)} %collective-permute-done.8.refs_11_), channel_id=1, source_target_pairs={{0,24},{8,0},{16,8},{24,16},{1,25},{9,1},{17,9},{25,17},{2,26},{10... | collective-permute-start | bytes 589832 | tf_op jit(solution)/shard_map/ppermute | solution.py:350
  45.8 2.6 %collective-permute-start.22 = (f32[8,256]{1,0:T(8,128)S(1)}, f32[8,256]{1,0:T(8,128)S(1)}, u32[]{:S(2)}, u32[]{:S(2)}) collective-permute-start(f32[8,256]{1,0:T(8,128)S(1)} %get-tuple-element.41), channel_id=1, source_target_pairs={{0,32},{32,0},{64,96},{96,64},{1,33},{33,1},{65,97},{97,65},{2,34}... | collective-permute-start | bytes 24584 | tf_op jit(solution)/shard_map/ppermute | solution.py:249
  45.9 6.5 %collective-permute-start.23 = (f32[8,256]{1,0:T(8,128)S(1)}, f32[8,256]{1,0:T(8,128)S(1)}, u32[]{:S(2)}, u32[]{:S(2)}) collective-permute-start(f32[8,256]{1,0:T(8,128)S(1)} %get-tuple-element.41), channel_id=1, source_target_pairs={{0,0},{32,64},{64,32},{96,96},{1,1},{33,65},{65,33},{97,97},{2,2},... | collective-permute-start | bytes 24584 | tf_op jit(solution)/shard_map/ppermute | solution.py:249
  47.8 11.3 %collective-permute-start.17 = (bf16[2,768,128]{2,1,0:T(8,128)(2,1)S(1)}, bf16[2,768,128]{2,1,0:T(8,128)(2,1)S(1)}, u32[]{:S(2)}, u32[]{:S(2)}) collective-permute-start(bf16[2,768,128]{2,1,0:T(8,128)(2,1)S(1)} %collective-permute-done.13.refs_5_), channel_id=1, source_target_pairs={{0,32},{32,0},{64,96},{96,64},{1,33},{33,1},{65,97},{97,65},{2,34}... | collective-permute-start | bytes 1179656 | tf_op jit(solution)/shard_map/ppermute | solution.py:357
  47.9 11.2 %collective-permute-start.18 = (bf16[2,768,128]{2,1,0:T(8,128)(2,1)S(1)}, bf16[2,768,128]{2,1,0:T(8,128)(2,1)S(1)}, u32[]{:S(2)}, u32[]{:S(2)}) collective-permute-start(bf16[2,768,128]{2,1,0:T(8,128)(2,1)S(1)} %collective-permute-done.14.refs_6_), channel_id=1, source_target_pairs={{0,32},{32,0},{64,96},{96,64},{1,33},{33,1},{65,97},{97,65},{2,34}... | collective-permute-start | bytes 1179656 | tf_op jit(solution)/shard_map/ppermute | solution.py:357
  52.4 5.0 %collective-permute-start.24 = (f32[24,256]{1,0:T(8,128)S(1)}, f32[24,256]{1,0:T(8,128)S(1)}, u32[]{:S(2)}, u32[]{:S(2)}) collective-permute-start(f32[24,256]{1,0:T(8,128)S(1)} %constant_dynamic-update-slice_fusion.refs_16_), channel_id=1, source_target_pairs={{0,8},{8,16},{16,24},{24,0},{1,9},{9,17},{17,25},{25,1},{2,10},{10... | collective-permute-start | bytes 73736 | tf_op jit(solution)/shard_map/ppermute | solution.py:250
  52.4 5.0 %collective-permute-start.25 = (f32[24,256]{1,0:T(8,128)S(1)}, f32[24,256]{1,0:T(8,128)S(1)}, u32[]{:S(2)}, u32[]{:S(2)}) collective-permute-start(f32[24,256]{1,0:T(8,128)S(1)} %constant_dynamic-update-slice_fusion.refs_16_), channel_id=1, source_target_pairs={{0,24},{8,0},{16,8},{24,16},{1,25},{9,1},{17,9},{25,17},{2,26},{10... | collective-permute-start | bytes 73736 | tf_op jit(solution)/shard_map/ppermute | solution.py:250
  55.6 2.3 %collective-permute-start.19 = (bf16[768,128]{1,0:T(8,128)(2,1)S(1)}, bf16[768,128]{1,0:T(8,128)(2,1)S(1)}, u32[]{:S(2)}, u32[]{:S(2)}) collective-permute-start(bf16[768,128]{1,0:T(8,128)(2,1)S(1)} %collective-permute-done.8.refs_11_), channel_id=1, source_target_pairs={{0,32},{32,0},{64,96},{96,64},{1,33},{33,1},{65,97},{97,65},{2,34}... | collective-permute-start | bytes 589832 | tf_op jit(solution)/shard_map/ppermute | solution.py:358
  (14 other events, 184.2 us)
